TPU v7x, 128 devices: a whole 4x4x4 slice. The times are simulated.
128 devices in a mesh: col: 4 (over x_hi, core), row: 32 (over z, y, x_lo).
Axes of the slice: x: 4 (x_hi: 2, x_lo: 2; x = x_hi * 2 + x_lo), y: 4, z: 4, core: 2. Of those that a mesh axis runs over, the one named last changes fastest.
Arguments:
- amplitudes: bfloat16 [2, 32, 1536, 1536], P(None, 'row', None, 'col'), may hold values from -6 to 6
- coupling: bfloat16 [2, 1536, 4, 1536], P(None, 'row', None, 'col'), may hold values from -0.109375 to 0.109375
Outputs:
- cycle_term: bfloat16 [32, 1536, 4, 1536], P(None, 'row', None, 'col')
All inputs are finite; a program needn't handle non-finite values.
Results may differ from a plain program's by a relative error of at most 0.001.
Values may be sent and summed in bfloat16 or wider, within the bound.
No kernel may reach another device: no remote copies, remote signals or barrier semaphores. Data moves between devices by JAX's collectives and lax.ppermute only.
A program may use at most 128 MiB of HBM per device.

v0:
```python
import jax
import jax.numpy as jnp
from jax import lax
from jax.sharding import PartitionSpec as P


def contract(pairs, coupling):
    whole = lax.all_gather(coupling, "row", axis=1, tiled=True)
    result = jnp.einsum("ijba,iakc->jbkc", pairs, whole, preferred_element_type=jnp.float32)
    return result.astype(jnp.bfloat16)


def on_device(amplitudes, coupling):
    full_pairs = lax.all_gather(amplitudes, "col", axis=3, tiled=True)
    relaid = lax.all_to_all(full_pairs, "row", split_axis=2, concat_axis=1, tiled=True)
    return contract(relaid, coupling)


def solution(mesh):
    placed = (P(None, "row", None, "col"), P(None, "row", None, "col"))
    return jax.shard_map(
        on_device,
        mesh=mesh,
        in_specs=placed,
        out_specs=P(None, "row", None, "col"),
        check_vma=False,
    )
```

profile of v0, /device:TPU:1, one launch (start us, length us, event | category | flops | bytes accessed | tf_op | source)
XLA Modules:
  0.0 463.2 jit_solution(6549823937306464217)
XLA Ops:
  6.5 0.0 all-gather.3.cloned.1.call-start
  6.5 14.9 %copy.9 = bf16[2,1,1536,384]{3,0,1,2:T(2,128)(2,1)} copy(bf16[2,1,1536,384]{3,2,1,0:T(8,128)(2,1)} %param.2) | data formatting | bytes 4718592 | tf_op args[0]
  21.4 0.0 all-gather.3.cloned.1.call-update
  21.5 0.0 all-gather.5.cloned.1.call-start
  21.5 1.7 copy.11
  23.2 0.0 all-gather.5.cloned.1.call-update
  23.2 71.8 %all-gather.3.cloned.1.call-done = bf16[2,1,1536,1536]{3,0,1,2:T(2,128)(2,1)} async-done(((bf16[2,1,1536,384]{3,0,1,2:T(2,128)(2,1)}), bf16[2,1,1536,1536]{3,0,1,2:T(2,128)(2,1)}) %all-gather.3.cloned.1.call-update) | async-done | bytes 9437200 | tf_op jit(solution)/shard_map/all_gather | solution.py:14
  95.1 7.1 %all-to-all-start = ((bf16[2,1,1536,1536]{3,0,1,2:T(2,128)(2,1)}), bf16[2,1,1536,1536]{3,0,1,2:T(2,128)(2,1)}, u32[]{:S(2)}, u32[]{:S(2)}) async-start(bf16[2,1,1536,1536]{3,0,1,2:T(2,128)(2,1)} %all-gather.3.cloned.1.call-done), calls=%async_computation | async-start | bytes 18874368 | tf_op jit(solution)/shard_map/all_to_all | solution.py:15
  102.2 329.2 %all-gather.5.cloned.1.call-done = bf16[2,1536,4,384]{3,1,0,2:T(8,128)(2,1)} async-done(((bf16[2,48,4,384]{3,1,0,2:T(8,128)(2,1)}), bf16[2,1536,4,384]{3,1,0,2:T(8,128)(2,1)}) %all-gather.5.cloned.1.call-update) | async-done | bytes 9437200 | tf_op jit(solution)/shard_map/all_gather | solution.py:8
  431.4 0.0 all-to-all-done
  431.4 20.3 %bitcast_convert_fusion = bf16[32,48,4,384]{3,1,2,0:T(8,128)(2,1)S(1)} fusion(bf16[2,1536,4,384]{3,1,0,2:T(8,128)(2,1)} %all-gather.5.cloned.1.call-done, bf16[2,32,48,1536,1]{3,0,2,1,4:T(2,128)(2,1)} %bitcast.1), kind=kOutput, calls=%fused_computation | convolution fusion | flops 14497873920 | bytes 23592960 | tf_op jit(solution)/shard_map/ijba,iakc->jbkc/dot_general | solution.py:9
  451.8 4.5 copy.13
Async XLA Ops:
  6.5 88.5 %all-gather.3.cloned.1.call-start = ((), (), s32[]{:S(2)}) async-start(), calls=%async_computation.1 | async-start | bytes 11796480 | tf_op jit(solution)/shard_map/all_gather | solution.py:14
  21.5 410.0 %all-gather.5.cloned.1.call-start = ((), (), s32[]{:S(2)}) async-start(), calls=%async_computation.2 | async-start | bytes 9732096 | tf_op jit(solution)/shard_map/all_gather | solution.py:8
  95.1 336.3 %all-to-all-start = ((bf16[2,1,1536,1536]{3,0,1,2:T(2,128)(2,1)}), bf16[2,1,1536,1536]{3,0,1,2:T(2,128)(2,1)}, u32[]{:S(2)}, u32[]{:S(2)}) async-start(bf16[2,1,1536,1536]{3,0,1,2:T(2,128)(2,1)} %all-gather.3.cloned.1.call-done), calls=%async_computation | async-start | bytes 18874368 | tf_op jit(solution)/shard_map/all_to_all | solution.py:15
Sparse Core Ops, SparseCore 0:
  21.6 73.4 all-gather.2
  96.7 334.6 all-gather.4
where the time goes:
time: 463 us
  waiting for transfers between devices  401 us (87%)
  local copies, waits for them, and re-layouts  21.2 us (5%)
  matrix products  20.3 us (4%)
  between operations  13.4 us (3%)
  starting transfers between devices  7.15 us (2%)
    all_gather x1, waiting for transfers between devices, contract(): whole = lax.all_gather(coupling, 'row', axis=1, tiled=True)  329 us
    all_gather x1, waiting for transfers between devices, on_device(): full_pairs = lax.all_gather(amplitudes, 'col', axis=3, tiled=True)  71.8 us
    dot_general x1, matrix products, contract(): jnp.einsum('ijba,iakc->jbkc', pairs, whole, preferred_element_type=jnp.fl...  20.3 us
    unnamed x2, local copies, waits for them, and re-layouts  16.6 us
  transfers between devices with their start and end apart: 3, of which 2 were waited for; matrix products, arithmetic and copies ran while one was open for 0% of the time, Pallas kernels for 0%

commit v1 on v0

v1 whole, which is shorter than its diff:
```python
import jax
import jax.numpy as jnp
from jax import lax
from jax.sharding import Mesh, PartitionSpec as P

FINE = ("xh", "core", "z", "y", "xl")
ROW = ("z", "y", "xl")
SWAP = [(0, 1), (1, 0)]


def on_device(amplitudes, coupling):
    ni, _, v, qa = amplitudes.shape
    rows = lax.axis_size(ROW)
    nb = v // rows
    na, nk, qc = coupling.shape[1:]
    xh, core = lax.axis_index("xh"), lax.axis_index("core")

    mine = jnp.transpose(coupling, (2, 0, 1, 3))
    other = lax.ppermute(mine, "xl", SWAP)
    first = lax.axis_index("xl") == 0
    pair = jnp.concatenate([jnp.where(first, mine, other), jnp.where(first, other, mine)], axis=2)
    whole = lax.all_gather(pair[None], ("z", "y"), axis=0, tiled=True)
    whole = whole.reshape((4, 4) + pair.shape)

    total = None
    own, far = [], []
    for i in range(ni):
        chunks = amplitudes[i, 0].reshape(rows, nb, qa)
        got = lax.all_to_all(chunks, ROW, split_axis=0, concat_axis=0, tiled=True)
        away = lax.ppermute(got, "xh", SWAP)
        own.append((got, lax.ppermute(got, "core", SWAP)))
        far.append((away, lax.ppermute(away, "core", SWAP)))
    for half, there in ((own, xh), (far, 1 - xh)):
        for i in range(ni):
            for block, c in zip(half[i], (core, 1 - core)):
                matrix = lax.dynamic_index_in_dim(whole, 2 * there + c, 0, keepdims=False)[:, :, i]
                matrix = jnp.transpose(matrix, (0, 2, 1, 3)).reshape(qa, nk, qc)
                term = jnp.einsum("jba,akc->jbkc", block, matrix, preferred_element_type=jnp.float32)
                total = term if total is None else total + term
    return total.astype(jnp.bfloat16)


def solution(mesh):
    fine = Mesh(mesh.devices.reshape(2, 2, 4, 4, 2), FINE)
    placed = P(None, ROW, None, ("xh", "core"))
    return jax.shard_map(
        on_device, mesh=fine, in_specs=(placed, placed), out_specs=placed, check_vma=False
    )
```

time: 463 us -> 212 us (0.46)
  waiting for transfers between devices: 401 us -> 46.9 us
  matrix products: 20.3 us -> 67.1 us
  blocking collectives: 0 us -> 29.1 us
  starting transfers between devices: 7.15 us -> 34.3 us
    all_gather x2 -> x1, waiting for transfers between devices: 401 us -> 0.01 us  [on_device(): whole = lax.all_gather(pair[None], ('z', 'y'), axis=0, tiled=True)]
    dot_general x1 -> x8, matrix products: 20.3 us -> 67.1 us  [on_device(): jnp.einsum('jba,akc->jbkc', block, matrix, preferred_element_type=jnp.flo...]
    ppermute x0 -> x7, waiting for transfers between devices: none -> 33.6 us  [the longest x2 27.3 us: on_device(): away = lax.ppermute(got, 'xh', SWAP)]
    all_to_all x0 -> x1, blocking collectives: none -> 29.1 us  [on_device(): got = lax.all_to_all(chunks, ROW, split_axis=0, concat_axis=0, tiled=True)]
    ppermute x0 -> x7, starting transfers between devices: none -> 28.8 us  [the longest x2 12.8 us: on_device(): far.append((away, lax.ppermute(away, 'core', SWAP)))]
    unnamed x2 -> x3, local copies, waits for them, and re-layouts: 16.6 us -> 1 us
    all_to_all x1, waiting for transfers between devices: 0.01 us -> 13.4 us  [on_device(): got = lax.all_to_all(chunks, ROW, split_axis=0, concat_axis=0, tiled=True)]
    dynamic_slice x0 -> x1, local copies, waits for them, and re-layouts: none -> 5.23 us  [on_device(): lax.dynamic_index_in_dim(whole, 2 * there + c, 0, keepdims=False)[:, :, i]]
  transfers between devices with their start and end apart: 3 -> 9, of which waited for: 2 -> 4; matrix products, arithmetic and copies ran while one was open for 0% -> 24% of each run, Pallas kernels for 0% -> 0%
where the time goes in v1:
time: 212 us; the launch traced here: 211 us
  matrix products  67.1 us (32%)
  waiting for transfers between devices  46.9 us (22%)
  starting transfers between devices  34.3 us (16%)
  blocking collectives  29.1 us (14%)
  local copies, waits for them, and re-layouts  18.3 us (9%)
  between operations  13.5 us (6%)
    dot_general x8, matrix products, on_device(): jnp.einsum('jba,akc->jbkc', block, matrix, preferred_element_type=jnp.flo...  67.1 us
    all_to_all x1, blocking collectives, on_device(): got = lax.all_to_all(chunks, ROW, split_axis=0, concat_axis=0, tiled=True)  29.1 us
    ppermute x2, waiting for transfers between devices, on_device(): away = lax.ppermute(got, 'xh', SWAP)  27.3 us
    all_to_all x1, waiting for transfers between devices, on_device(): got = lax.all_to_all(chunks, ROW, split_axis=0, concat_axis=0, tiled=True)  13.4 us
    ppermute x2, starting transfers between devices, on_device(): far.append((away, lax.ppermute(away, 'core', SWAP)))  12.8 us
    ppermute x2, starting transfers between devices, on_device(): own.append((got, lax.ppermute(got, 'core', SWAP)))  8.84 us
    convert_element_type x1, local copies, waits for them, and re-layouts, on_device(): return total.astype(jnp.bfloat16)  8.16 us
    ppermute x1, waiting for transfers between devices, on_device(): other = lax.ppermute(mine, 'xl', SWAP)  6.22 us
  transfers between devices with their start and end apart: 9, of which 4 were waited for; matrix products, arithmetic and copies ran while one was open for 24% of the time, Pallas kernels for 0%

profile of v1, /device:TPU:1, one launch (start us, length us, event | category | flops | bytes accessed | tf_op | source)
XLA Modules:
  0.0 211.2 jit_solution(5855531848090889004)
XLA Ops:
  7.5 2.1 %collective-permute-start = (bf16[4,2,48,384]{3,2,1,0:T(8,128)(2,1)S(1)}, bf16[4,2,48,384]{3,2,1,0:T(8,128)(2,1)S(1)}, u32[]{:S(2)}, u32[]{:S(2)}) collective-permute-start(bf16[4,2,48,384]{3,2,1,0:T(8,128)(2,1)S(1)} %bitcast.134), channel_id=1, source_target_pairs={{0,1},{1,0},{2,3},{3,2},{4,5},{5,4},{6,7},{7,6},{8,9},{9,8},{10,11... | collective-permute-start | bytes 884744 | tf_op jit(solution)/shard_map/ppermute | solution.py:19
  9.7 6.2 %collective-permute-done = bf16[4,2,48,384]{3,2,1,0:T(8,128)(2,1)S(1)} collective-permute-done((bf16[4,2,48,384]{3,2,1,0:T(8,128)(2,1)S(1)}, bf16[4,2,48,384]{3,2,1,0:T(8,128)(2,1)S(1)}, u32[]{:S(2)}, u32[]{:S(2)}) %collective-permute-start) | collective-permute-done | bytes 294944 | tf_op jit(solution)/shard_map/ppermute | solution.py:19
  15.9 1.2 broadcast_select_fusion.1
  18.0 1.3 fusion.20
  19.3 29.1 %all_to_all.10 = bf16[32,48,384]{2,1,0:T(8,128)(2,1)S(1)} all-to-all(bf16[32,48,384]{2,1,0:T(8,128)(2,1)S(1)} %bitcast.132), channel_id=1, replica_groups=mesh['xh'=2,'core'=2,'z'=4,'y'=4,'xl'=2] {'z','y','xl'}, dimensions={0} | all-to-all | bytes 2359296 | tf_op jit(solution)/shard_map/all_to_all | solution.py:29
  48.3 5.4 %all-to-all-start.1 = ((bf16[32,48,384]{2,1,0:T(8,128)(2,1)}), bf16[32,48,384]{2,1,0:T(8,128)(2,1)S(1)}, u32[]{:S(2)}, u32[]{:S(2)}) async-start(bf16[32,48,384]{2,1,0:T(8,128)(2,1)} %bitcast.22), calls=%async_computation.1 | async-start | bytes 2359296 | tf_op jit(solution)/shard_map/all_to_all | solution.py:29
  53.8 2.6 %collective-permute-start.3 = (bf16[32,48,384]{2,1,0:T(8,128)(2,1)S(1)}, bf16[32,48,384]{2,1,0:T(8,128)(2,1)}, u32[]{:S(2)}, u32[]{:S(2)}) collective-permute-start(bf16[32,48,384]{2,1,0:T(8,128)(2,1)S(1)} %all_to_all.10), channel_id=1, source_target_pairs={{0,64},{64,0},{1,65},{65,1},{2,66},{66,2},{3,67},{67,3},{4,68},{68... | collective-permute-start | bytes 3538952 | tf_op jit(solution)/shard_map/ppermute | solution.py:30
  56.3 13.4 %all-to-all-done.1 = bf16[32,48,384]{2,1,0:T(8,128)(2,1)S(1)} async-done(((bf16[32,48,384]{2,1,0:T(8,128)(2,1)}), bf16[32,48,384]{2,1,0:T(8,128)(2,1)S(1)}, u32[]{:S(2)}, u32[]{:S(2)}) %all-to-all-start.1) | async-done | bytes 1179680 | tf_op jit(solution)/shard_map/all_to_all | solution.py:29
  69.7 2.5 %collective-permute-start.5 = (bf16[32,48,384]{2,1,0:T(8,128)(2,1)S(1)}, bf16[32,48,384]{2,1,0:T(8,128)(2,1)}, u32[]{:S(2)}, u32[]{:S(2)}) collective-permute-start(bf16[32,48,384]{2,1,0:T(8,128)(2,1)S(1)} %all-to-all-done.1), channel_id=1, source_target_pairs={{0,64},{64,0},{1,65},{65,1},{2,66},{66,2},{3,67},{67,3},{4,68},{68... | collective-permute-start | bytes 3538952 | tf_op jit(solution)/shard_map/ppermute | solution.py:30
  72.2 8.8 %collective-permute-start.1 = (bf16[32,48,384]{2,1,0:T(8,128)(2,1)S(1)}, bf16[32,48,384]{2,1,0:T(8,128)(2,1)}, u32[]{:S(2)}, u32[]{:S(2)}) collective-permute-start(bf16[32,48,384]{2,1,0:T(8,128)(2,1)S(1)} %all_to_all.10), channel_id=1, source_target_pairs={{0,32},{32,0},{1,33},{33,1},{2,34},{34,2},{3,35},{35,3},{4,36},{36... | collective-permute-start | bytes 3538952 | tf_op jit(solution)/shard_map/ppermute | solution.py:31
  81.0 10.5 %collective-permute-done.3 = bf16[32,48,384]{2,1,0:T(8,128)(2,1)} collective-permute-done((bf16[32,48,384]{2,1,0:T(8,128)(2,1)S(1)}, bf16[32,48,384]{2,1,0:T(8,128)(2,1)}, u32[]{:S(2)}, u32[]{:S(2)}) %collective-permute-start.3) | collective-permute-done | bytes 1179680 | tf_op jit(solution)/shard_map/ppermute | solution.py:30
  91.5 8.4 %collective-permute-start.4 = (bf16[32,48,384]{2,1,0:T(8,128)(2,1)}, bf16[32,48,384]{2,1,0:T(8,128)(2,1)}, u32[]{:S(2)}, u32[]{:S(2)}) collective-permute-start(bf16[32,48,384]{2,1,0:T(8,128)(2,1)} %collective-permute-done.3), channel_id=1, source_target_pairs={{0,32},{32,0},{1,33},{33,1},{2,34},{34,2},{3,35},{35,3},{4,36},{36... | collective-permute-start | bytes 3538952 | tf_op jit(solution)/shard_map/ppermute | solution.py:32
  99.9 16.9 %collective-permute-done.5 = bf16[32,48,384]{2,1,0:T(8,128)(2,1)} collective-permute-done((bf16[32,48,384]{2,1,0:T(8,128)(2,1)S(1)}, bf16[32,48,384]{2,1,0:T(8,128)(2,1)}, u32[]{:S(2)}, u32[]{:S(2)}) %collective-permute-start.5) | collective-permute-done | bytes 1179680 | tf_op jit(solution)/shard_map/ppermute | solution.py:30
  116.7 4.4 %collective-permute-start.6 = (bf16[32,48,384]{2,1,0:T(8,128)(2,1)}, bf16[32,48,384]{2,1,0:T(8,128)(2,1)}, u32[]{:S(2)}, u32[]{:S(2)}) collective-permute-start(bf16[32,48,384]{2,1,0:T(8,128)(2,1)} %collective-permute-done.5), channel_id=1, source_target_pairs={{0,32},{32,0},{1,33},{33,1},{2,34},{34,2},{3,35},{35,3},{4,36},{36... | collective-permute-start | bytes 3538952 | tf_op jit(solution)/shard_map/ppermute | solution.py:32
  121.2 5.2 %constant_dynamic-slice_fusion.3 = (bf16[1,4,4,2,96,384]{5,4,3,2,1,0:T(8,128)(2,1)S(1)}, bf16[1,4,4,2,96,384]{5,4,3,2,1,0:T(8,128)(2,1)S(1)}, bf16[1,4,4,2,96,38...) fusion(bf16[4,4,4,2,96,384]{5,4,3,2,1,0:T(8,128)(2,1)} %bitcast.124, s32[]{:T(128)S(6)} %select_n.32, ...), kind=kLoop, calls=%fused_computation.28 | loop fusion | bytes 18874384 | tf_op jit(solution)/shard_map/jit(dynamic_index_in_dim)/dynamic_slice | solution.py:36
  128.6 6.5 %fusion.2 = f32[4,384,32,48]{1,3,2,0:T(8,128)} fusion(bf16[384,4,384,1]{2,0,3,1:T(8,128)(2,1)S(1)} %bitcast.131, bf16[32,48,384]{2,1,0:T(8,128)(2,1)} %collective-permute-done.5), kind=kOutput, calls=%fused_computation.7 | convolution fusion | flops 1811939328 | bytes 11796480 | tf_op jit(solution)/shard_map/jba,akc->jbkc/dot_general | solution.py:38
  135.1 6.3 %fusion.6 = f32[4,384,32,48]{1,3,2,0:T(8,128)} fusion(bf16[384,4,384,1]{2,0,3,1:T(8,128)(2,1)S(1)} %bitcast.130, bf16[32,48,384]{2,1,0:T(8,128)(2,1)} %collective-permute-done.3), kind=kOutput, calls=%fused_computation.11 | convolution fusion | flops 1811939328 | bytes 11796480 | tf_op jit(solution)/shard_map/jba,akc->jbkc/dot_general | solution.py:38
  141.4 5.1 %fusion.14 = f32[4,384,32,48]{1,3,2,0:T(8,128)} fusion(bf16[384,4,384,1]{2,0,3,1:T(8,128)(2,1)S(1)} %bitcast.126, bf16[32,48,384]{2,1,0:T(8,128)(2,1)S(1)} %all_to_all.10), kind=kOutput, calls=%fused_computation.19 | convolution fusion | flops 1811939328 | bytes 11796480 | tf_op jit(solution)/shard_map/jba,akc->jbkc/dot_general | solution.py:38
  146.5 5.1 %fusion.10 = f32[4,384,32,48]{1,3,2,0:T(8,128)} fusion(bf16[384,4,384,1]{2,0,3,1:T(8,128)(2,1)S(1)} %bitcast.125, bf16[32,48,384]{2,1,0:T(8,128)(2,1)S(1)} %all-to-all-done.1), kind=kOutput, calls=%fused_computation.15 | convolution fusion | flops 1811939328 | bytes 11796480 | tf_op jit(solution)/shard_map/jba,akc->jbkc/dot_general | solution.py:38
  151.9 6.3 %fusion.4 = f32[4,384,32,48]{1,3,2,0:T(8,128)} fusion(bf16[384,4,384,1]{2,0,3,1:T(8,128)(2,1)S(1)} %bitcast.128, bf16[32,48,384]{2,1,0:T(8,128)(2,1)} %collective-permute-done.4), kind=kOutput, calls=%fused_computation.9 | convolution fusion | flops 1811939328 | bytes 11796480 | tf_op jit(solution)/shard_map/jba,akc->jbkc/dot_general | solution.py:38
  158.5 6.2 %fusion.8 = f32[4,384,32,48]{1,3,2,0:T(8,128)} fusion(bf16[384,4,384,1]{2,0,3,1:T(8,128)(2,1)S(1)} %bitcast.129, bf16[32,48,384]{2,1,0:T(8,128)(2,1)} %collective-permute-done.2), kind=kOutput, calls=%fused_computation.13 | convolution fusion | flops 1811939328 | bytes 11796480 | tf_op jit(solution)/shard_map/jba,akc->jbkc/dot_general | solution.py:38
  164.7 6.2 %fusion.12 = f32[4,384,32,48]{1,3,2,0:T(8,128)} fusion(bf16[384,4,384,1]{2,0,3,1:T(8,128)(2,1)S(1)} %bitcast.127, bf16[32,48,384]{2,1,0:T(8,128)(2,1)} %collective-permute-done.1), kind=kOutput, calls=%fused_computation.17 | convolution fusion | flops 1811939328 | bytes 11796480 | tf_op jit(solution)/shard_map/jba,akc->jbkc/dot_general | solution.py:38
  171.0 25.3 %fusion = bf16[32,48,4,384]{3,1,0,2:T(8,128)(2,1)} fusion(f32[4,384,32,48]{1,3,2,0:T(8,128)} %fusion.2, f32[4,384,32,48]{1,3,2,0:T(8,128)} %fusion.4, f32[4,384,32,48]{1,3,2,0:T(8,128)} %fusion.6, f32[4,384,32,48]{1,3,2,0:T(8,128)} %fusion.8, f32[4,384,32,48]{1,3,2,0:T(8,128)} %fusion.10, f32[4,384,32,48]{1,3,2,0:T(8,128)} %fusion.14, ...), kind=kOutput, calls=%fused_computation.1 | convolution fusion | flops 1830813696 | bytes 73138176 | tf_op jit(solution)/shard_map/jba,akc->jbkc/dot_general | solution.py:38
  196.2 8.2 %copy.13 = bf16[32,48,4,384]{3,2,1,0:T(4,128)(2,1)} copy(bf16[32,48,4,384]{3,1,0,2:T(8,128)(2,1)} %fusion) | data formatting | bytes 9437184 | tf_op jit(solution)/shard_map/convert_element_type | solution.py:40
  (18 shorter events, 4.5 us)
Async XLA Ops:
  6.5 114.6 %all-gather.3.cloned.1.call-start = ((), (), s32[]{:S(2)}) async-start(), calls=%async_computation.2 | async-start | bytes 10027008 | tf_op jit(solution)/shard_map/all_gather | solution.py:22
  7.5 8.3 %collective-permute-start = (bf16[4,2,48,384]{3,2,1,0:T(8,128)(2,1)S(1)}, bf16[4,2,48,384]{3,2,1,0:T(8,128)(2,1)S(1)}, u32[]{:S(2)}, u32[]{:S(2)}) collective-permute-start(bf16[4,2,48,384]{3,2,1,0:T(8,128)(2,1)S(1)} %bitcast.134), channel_id=1, source_target_pairs={{0,1},{1,0},{2,3},{3,2},{4,5},{5,4},{6,7},{7,6},{8,9},{9,8},{10,11... | collective-permute-start | bytes 884744 | tf_op jit(solution)/shard_map/ppermute | solution.py:19
  15.9 2.1 %copy-start = (bf16[2,1,1536,384]{3,2,1,0:T(8,128)(2,1)S(1)}, bf16[2,1,1536,384]{3,2,1,0:T(8,128)(2,1)}, u32[]{:S(2)}) copy-start(bf16[2,1,1536,384]{3,2,1,0:T(8,128)(2,1)} %param.2) | copy-start | bytes 7077892
  48.3 21.4 %all-to-all-start.1 = ((bf16[32,48,384]{2,1,0:T(8,128)(2,1)}), bf16[32,48,384]{2,1,0:T(8,128)(2,1)S(1)}, u32[]{:S(2)}, u32[]{:S(2)}) async-start(bf16[32,48,384]{2,1,0:T(8,128)(2,1)} %bitcast.22), calls=%async_computation.1 | async-start | bytes 2359296 | tf_op jit(solution)/shard_map/all_to_all | solution.py:29
  53.8 37.7 %collective-permute-start.3 = (bf16[32,48,384]{2,1,0:T(8,128)(2,1)S(1)}, bf16[32,48,384]{2,1,0:T(8,128)(2,1)}, u32[]{:S(2)}, u32[]{:S(2)}) collective-permute-start(bf16[32,48,384]{2,1,0:T(8,128)(2,1)S(1)} %all_to_all.10), channel_id=1, source_target_pairs={{0,64},{64,0},{1,65},{65,1},{2,66},{66,2},{3,67},{67,3},{4,68},{68... | collective-permute-start | bytes 3538952 | tf_op jit(solution)/shard_map/ppermute | solution.py:30
  69.7 47.1 %collective-permute-start.5 = (bf16[32,48,384]{2,1,0:T(8,128)(2,1)S(1)}, bf16[32,48,384]{2,1,0:T(8,128)(2,1)}, u32[]{:S(2)}, u32[]{:S(2)}) collective-permute-start(bf16[32,48,384]{2,1,0:T(8,128)(2,1)S(1)} %all-to-all-done.1), channel_id=1, source_target_pairs={{0,64},{64,0},{1,65},{65,1},{2,66},{66,2},{3,67},{67,3},{4,68},{68... | collective-permute-start | bytes 3538952 | tf_op jit(solution)/shard_map/ppermute | solution.py:30
  72.2 92.5 %collective-permute-start.1 = (bf16[32,48,384]{2,1,0:T(8,128)(2,1)S(1)}, bf16[32,48,384]{2,1,0:T(8,128)(2,1)}, u32[]{:S(2)}, u32[]{:S(2)}) collective-permute-start(bf16[32,48,384]{2,1,0:T(8,128)(2,1)S(1)} %all_to_all.10), channel_id=1, source_target_pairs={{0,32},{32,0},{1,33},{33,1},{2,34},{34,2},{3,35},{35,3},{4,36},{36... | collective-permute-start | bytes 3538952 | tf_op jit(solution)/shard_map/ppermute | solution.py:31
  81.0 77.4 %collective-permute-start.2 = (bf16[32,48,384]{2,1,0:T(8,128)(2,1)S(1)}, bf16[32,48,384]{2,1,0:T(8,128)(2,1)}, u32[]{:S(2)}, u32[]{:S(2)}) collective-permute-start(bf16[32,48,384]{2,1,0:T(8,128)(2,1)S(1)} %all-to-all-done.1), channel_id=1, source_target_pairs={{0,32},{32,0},{1,33},{33,1},{2,34},{34,2},{3,35},{35,3},{4,36},{36... | collective-permute-start | bytes 3538952 | tf_op jit(solution)/shard_map/ppermute | solution.py:31
  91.5 60.4 %collective-permute-start.4 = (bf16[32,48,384]{2,1,0:T(8,128)(2,1)}, bf16[32,48,384]{2,1,0:T(8,128)(2,1)}, u32[]{:S(2)}, u32[]{:S(2)}) collective-permute-start(bf16[32,48,384]{2,1,0:T(8,128)(2,1)} %collective-permute-done.3), channel_id=1, source_target_pairs={{0,32},{32,0},{1,33},{33,1},{2,34},{34,2},{3,35},{35,3},{4,36},{36... | collective-permute-start | bytes 3538952 | tf_op jit(solution)/shard_map/ppermute | solution.py:32
  116.7 54.2 %collective-permute-start.6 = (bf16[32,48,384]{2,1,0:T(8,128)(2,1)}, bf16[32,48,384]{2,1,0:T(8,128)(2,1)}, u32[]{:S(2)}, u32[]{:S(2)}) collective-permute-start(bf16[32,48,384]{2,1,0:T(8,128)(2,1)} %collective-permute-done.5), channel_id=1, source_target_pairs={{0,32},{32,0},{1,33},{33,1},{2,34},{34,2},{3,35},{35,3},{4,36},{36... | collective-permute-start | bytes 3538952 | tf_op jit(solution)/shard_map/ppermute | solution.py:32
Sparse Core Ops, SparseCore 0:
  18.1 91.6 all-gather.2

commit v2 on v1

v2 whole, which is shorter than its diff:
```python
import jax
import jax.numpy as jnp
from jax import lax
from jax.experimental import pallas as pl
from jax.experimental.pallas import tpu as pltpu
from jax.sharding import Mesh, PartitionSpec as P

FINE = ("xh", "core", "z", "y", "xl")
ROW = ("z", "y", "xl")
SWAP = [(0, 1), (1, 0)]
TILE = 192


def contract_kernel(place, *refs):
    blocks, (w, out, lhs, mat, total, staged, lsem, wsem, osem) = refs[:8], refs[8:]
    rows, qa = blocks[0].shape
    tiles = rows // TILE
    nk, qc = out.shape[1:]
    xh, core = place[0], place[1]
    steps = [(i, far) for far in (0, 1) for i in (0, 1)]

    def copies(s):
        i, far = steps[s]
        slot = s % 2
        half = 1 - xh if far else xh
        mine, other = blocks[4 * i + 2 * far], blocks[4 * i + 2 * far + 1]
        first = pl.multiple_of(core * qa, 128)
        second = pl.multiple_of((1 - core) * qa, 128)
        return (
            pltpu.make_async_copy(mine, lhs.at[slot, :, pl.ds(first, qa)], lsem.at[slot, 0]),
            pltpu.make_async_copy(other, lhs.at[slot, :, pl.ds(second, qa)], lsem.at[slot, 1]),
            pltpu.make_async_copy(w.at[pl.ds(2 * half, 2), :, i], mat.at[slot], wsem.at[slot]),
        )

    def store(m):
        return pltpu.make_async_copy(
            staged.at[pl.ds(m * TILE, TILE)], out.at[pl.ds(m * TILE, TILE)], osem.at[m]
        )

    for c in copies(0):
        c.start()
    for s in range(len(steps)):
        if s + 1 < len(steps):
            for c in copies(s + 1):
                c.start()
        for c in copies(s):
            c.wait()
        slot = s % 2

        def tile(m, carry, s=s, slot=slot):
            at = pl.ds(pl.multiple_of(m * TILE, TILE), TILE)
            matrix = mat[slot].reshape(2 * qa, nk * qc)
            term = jnp.dot(lhs[slot, at, :], matrix, preferred_element_type=jnp.float32)
            if s:
                term = term + total[at, :]
            if s + 1 < len(steps):
                total[at, :] = term
            else:
                for k in range(nk):
                    staged[at, k, :] = term[:, k * qc : (k + 1) * qc].astype(staged.dtype)
                store(m).start()
            return carry

        lax.fori_loop(0, tiles, tile, 0)
    lax.fori_loop(0, tiles, lambda m, c: (store(m).wait(), c)[1], 0)


def contract(place, blocks, w, nk, qc):
    rows, qa = blocks[0].shape
    tiles = rows // TILE
    any_space = pl.BlockSpec(memory_space=pl.ANY)
    return pl.pallas_call(
        contract_kernel,
        out_shape=jax.ShapeDtypeStruct((rows, nk, qc), jnp.bfloat16),
        in_specs=[pl.BlockSpec(memory_space=pltpu.SMEM)] + [any_space] * 9,
        out_specs=any_space,
        scratch_shapes=[
            pltpu.VMEM((2, rows, 2 * qa), jnp.bfloat16),
            pltpu.VMEM((2, 2) + w.shape[1:2] + w.shape[3:], jnp.bfloat16),
            pltpu.VMEM((rows, nk * qc), jnp.float32),
            pltpu.VMEM((rows, nk, qc), jnp.bfloat16),
            pltpu.SemaphoreType.DMA((2, 2)),
            pltpu.SemaphoreType.DMA((2,)),
            pltpu.SemaphoreType.DMA((tiles,)),
        ],
        compiler_params=pltpu.CompilerParams(vmem_limit_bytes=48 << 20),
        cost_estimate=pl.CostEstimate(
            flops=2 * rows * 8 * qa * nk * qc, bytes_accessed=24 << 20, transcendentals=0
        ),
        name="contract",
    )(place, *blocks, w)


def on_device(amplitudes, coupling):
    ni, _, v, qa = amplitudes.shape
    rows = lax.axis_size(ROW)
    nb = v // rows
    na, nk, qc = coupling.shape[1:]

    mine = coupling.reshape(ni, na, nk * qc)
    other = lax.ppermute(mine, "xl", SWAP)
    first = lax.axis_index("xl") == 0
    pair = jnp.concatenate([jnp.where(first, mine, other), jnp.where(first, other, mine)], axis=1)
    whole = lax.all_gather(pair[None], ("z", "y"), axis=0, tiled=True)
    whole = whole.reshape((4, 4) + pair.shape)

    blocks = []
    for i in range(ni):
        chunks = amplitudes[i, 0].reshape(rows, nb, qa)
        got = lax.all_to_all(chunks, ROW, split_axis=0, concat_axis=0, tiled=True)
        away = lax.ppermute(got, "xh", SWAP)
        blocks += [got, lax.ppermute(got, "core", SWAP), away, lax.ppermute(away, "core", SWAP)]
    blocks = [b.reshape(rows * nb, qa) for b in blocks]
    place = jnp.stack([lax.axis_index("xh"), lax.axis_index("core")]).astype(jnp.int32)
    return contract(place, blocks, whole, nk, qc).reshape(rows, nb, nk, qc)


def solution(mesh):
    fine = Mesh(mesh.devices.reshape(2, 2, 4, 4, 2), FINE)
    placed = P(None, ROW, None, ("xh", "core"))
    return jax.shard_map(
        on_device, mesh=fine, in_specs=(placed, placed), out_specs=placed, check_vma=False
    )
```

time: 212 us -> 158 us (0.75)
  matrix products: 67.1 us -> 0 us
  Pallas kernels: 0 us -> 26.4 us
  local copies, waits for them, and re-layouts: 18.3 us -> 3.24 us
  waiting for transfers between devices: 46.9 us -> 50 us
    dot_general x8 -> x0, matrix products: 67.1 us -> none  [on_device(): jnp.einsum('jba,akc->jbkc', block, matrix, preferred_element_type=jnp.flo...]
    pallas_call x0 -> x1, Pallas kernels: none -> 26.4 us  [contract(): pl.pallas_call(contract_kernel, out_shape=jax.ShapeDtypeStruct((rows, nk,...]
    convert_element_type x1 -> x0, local copies, waits for them, and re-layouts: 8.16 us -> none  [on_device(): return total.astype(jnp.bfloat16)]
    dynamic_slice x1 -> x0, local copies, waits for them, and re-layouts: 5.23 us -> none  [on_device(): lax.dynamic_index_in_dim(whole, 2 * there + c, 0, keepdims=False)[:, :, i]]
    ppermute x4, waiting for transfers between devices: 0.01 us -> 2.53 us  [the longest x2 2.52 us: on_device(): lax.ppermute(away, 'core', SWAP)]
  transfers between devices with their start and end apart: 9 -> 9, of which waited for: 4 -> 5; matrix products, arithmetic and copies ran while one was open for 24% -> 1% of each run, Pallas kernels for 0% -> 0%
where the time goes in v2:
time: 158 us; the launch traced here: 157 us
  waiting for transfers between devices  50 us (32%)
  starting transfers between devices  34 us (22%)
  blocking collectives  29.3 us (19%)
  Pallas kernels  26.4 us (17%)
  between operations  13.4 us (8%)
  local copies, waits for them, and re-layouts  3.24 us (2%)
    all_to_all x1, blocking collectives, on_device(): got = lax.all_to_all(chunks, ROW, split_axis=0, concat_axis=0, tiled=True)  29.3 us
    ppermute x2, waiting for transfers between devices, on_device(): away = lax.ppermute(got, 'xh', SWAP)  27.8 us
    pallas_call x1, Pallas kernels, contract(): pl.pallas_call(contract_kernel, out_shape=jax.ShapeDtypeStruct((rows, nk,...  26.4 us
    all_to_all x1, waiting for transfers between devices, on_device(): got = lax.all_to_all(chunks, ROW, split_axis=0, concat_axis=0, tiled=True)  13.4 us
    ppermute x2, starting transfers between devices, on_device(): lax.ppermute(away, 'core', SWAP)  12.4 us
    ppermute x2, starting transfers between devices, on_device(): lax.ppermute(got, 'core', SWAP)  8.63 us
    ppermute x1, waiting for transfers between devices, on_device(): other = lax.ppermute(mine, 'xl', SWAP)  6.22 us
    all_to_all x1, starting transfers between devices, on_device(): got = lax.all_to_all(chunks, ROW, split_axis=0, concat_axis=0, tiled=True)  5.82 us
  transfers between devices with their start and end apart: 9, of which 5 were waited for; matrix products, arithmetic and copies ran while one was open for 1% of the time, Pallas kernels for 0%

profile of v2, /device:TPU:1, one launch (start us, length us, event | category | flops | bytes accessed | tf_op | source)
XLA Modules:
  0.0 157.3 jit_solution(8728966722964430044)
XLA Ops:
  6.5 1.1 reshape.41
  7.6 2.1 %collective-permute-start.6 = (bf16[2,48,1536]{2,1,0:T(8,128)(2,1)S(1)}, bf16[2,48,1536]{2,1,0:T(8,128)(2,1)S(1)}, u32[]{:S(2)}, u32[]{:S(2)}) collective-permute-start(bf16[2,48,1536]{2,1,0:T(8,128)(2,1)S(1)} %reshape.41), channel_id=1, source_target_pairs={{0,1},{1,0},{2,3},{3,2},{4,5},{5,4},{6,7},{7,6},{8,9},{9,8},{10,11... | collective-permute-start | bytes 884744 | tf_op jit(solution)/shard_map/ppermute | solution.py:101
  9.7 6.2 %collective-permute-done.6 = bf16[2,48,1536]{2,1,0:T(8,128)(2,1)S(1)} collective-permute-done((bf16[2,48,1536]{2,1,0:T(8,128)(2,1)S(1)}, bf16[2,48,1536]{2,1,0:T(8,128)(2,1)S(1)}, u32[]{:S(2)}, u32[]{:S(2)}) %collective-permute-start.6) | collective-permute-done | bytes 294944 | tf_op jit(solution)/shard_map/ppermute | solution.py:101
  16.0 0.9 pad_maximum_fusion
  16.9 0.0 all-gather.3.cloned.1.call-update
  16.9 0.9 copy-done
  17.8 1.2 fusion
  19.1 29.3 %all_to_all.10 = bf16[32,48,384]{2,1,0:T(8,128)(2,1)S(1)} all-to-all(bf16[32,48,384]{2,1,0:T(8,128)(2,1)S(1)} %bitcast.17), channel_id=1, replica_groups=mesh['xh'=2,'core'=2,'z'=4,'y'=4,'xl'=2] {'z','y','xl'}, dimensions={0} | all-to-all | bytes 2359296 | tf_op jit(solution)/shard_map/all_to_all | solution.py:110
  48.3 5.8 %all-to-all-start = ((bf16[32,48,384]{2,1,0:T(8,128)(2,1)}), bf16[32,48,384]{2,1,0:T(8,128)(2,1)S(1)}, u32[]{:S(2)}, u32[]{:S(2)}) async-start(bf16[32,48,384]{2,1,0:T(8,128)(2,1)} %bitcast.2), calls=%async_computation | async-start | bytes 2359296 | tf_op jit(solution)/shard_map/all_to_all | solution.py:110
  54.2 2.6 %collective-permute-start.4 = (bf16[32,48,384]{2,1,0:T(8,128)(2,1)S(1)}, bf16[32,48,384]{2,1,0:T(8,128)(2,1)}, u32[]{:S(2)}, u32[]{:S(2)}) collective-permute-start(bf16[32,48,384]{2,1,0:T(8,128)(2,1)S(1)} %all_to_all.10), channel_id=1, source_target_pairs={{0,64},{64,0},{1,65},{65,1},{2,66},{66,2},{3,67},{67,3},{4,68},{68... | collective-permute-start | bytes 3538952 | tf_op jit(solution)/shard_map/ppermute | solution.py:111
  56.7 13.4 %all-to-all-done = bf16[32,48,384]{2,1,0:T(8,128)(2,1)S(1)} async-done(((bf16[32,48,384]{2,1,0:T(8,128)(2,1)}), bf16[32,48,384]{2,1,0:T(8,128)(2,1)S(1)}, u32[]{:S(2)}, u32[]{:S(2)}) %all-to-all-start) | async-done | bytes 1179680 | tf_op jit(solution)/shard_map/all_to_all | solution.py:110
  70.2 2.5 %collective-permute-start.1 = (bf16[32,48,384]{2,1,0:T(8,128)(2,1)S(1)}, bf16[32,48,384]{2,1,0:T(8,128)(2,1)S(1)}, u32[]{:S(2)}, u32[]{:S(2)}) collective-permute-start(bf16[32,48,384]{2,1,0:T(8,128)(2,1)S(1)} %all-to-all-done), channel_id=1, source_target_pairs={{0,64},{64,0},{1,65},{65,1},{2,66},{66,2},{3,67},{67,3},{4,68},{68... | collective-permute-start | bytes 3538952 | tf_op jit(solution)/shard_map/ppermute | solution.py:111
  72.6 8.6 %collective-permute-start.3 = (bf16[32,48,384]{2,1,0:T(8,128)(2,1)S(1)}, bf16[32,48,384]{2,1,0:T(8,128)(2,1)}, u32[]{:S(2)}, u32[]{:S(2)}) collective-permute-start(bf16[32,48,384]{2,1,0:T(8,128)(2,1)S(1)} %all_to_all.10), channel_id=1, source_target_pairs={{0,32},{32,0},{1,33},{33,1},{2,34},{34,2},{3,35},{35,3},{4,36},{36... | collective-permute-start | bytes 3538952 | tf_op jit(solution)/shard_map/ppermute | solution.py:112
  81.3 0.0 collective-permute-start
  81.3 10.7 %collective-permute-done.4 = bf16[32,48,384]{2,1,0:T(8,128)(2,1)} collective-permute-done((bf16[32,48,384]{2,1,0:T(8,128)(2,1)S(1)}, bf16[32,48,384]{2,1,0:T(8,128)(2,1)}, u32[]{:S(2)}, u32[]{:S(2)}) %collective-permute-start.4) | collective-permute-done | bytes 1179680 | tf_op jit(solution)/shard_map/ppermute | solution.py:111
  92.0 8.1 %collective-permute-start.5 = (bf16[32,48,384]{2,1,0:T(8,128)(2,1)}, bf16[32,48,384]{2,1,0:T(8,128)(2,1)}, u32[]{:S(2)}, u32[]{:S(2)}) collective-permute-start(bf16[32,48,384]{2,1,0:T(8,128)(2,1)} %collective-permute-done.4), channel_id=1, source_target_pairs={{0,32},{32,0},{1,33},{33,1},{2,34},{34,2},{3,35},{35,3},{4,36},{36... | collective-permute-start | bytes 3538952 | tf_op jit(solution)/shard_map/ppermute | solution.py:112
  100.1 17.1 %collective-permute-done.1 = bf16[32,48,384]{2,1,0:T(8,128)(2,1)S(1)} collective-permute-done((bf16[32,48,384]{2,1,0:T(8,128)(2,1)S(1)}, bf16[32,48,384]{2,1,0:T(8,128)(2,1)S(1)}, u32[]{:S(2)}, u32[]{:S(2)}) %collective-permute-start.1) | collective-permute-done | bytes 1179680 | tf_op jit(solution)/shard_map/ppermute | solution.py:111
  117.2 4.3 %collective-permute-start.2 = (bf16[32,48,384]{2,1,0:T(8,128)(2,1)S(1)}, bf16[32,48,384]{2,1,0:T(8,128)(2,1)}, u32[]{:S(2)}, u32[]{:S(2)}) collective-permute-start(bf16[32,48,384]{2,1,0:T(8,128)(2,1)S(1)} %collective-permute-done.1), channel_id=1, source_target_pairs={{0,32},{32,0},{1,33},{33,1},{2,34},{34,2},{3,35},{35,3},{4,36},{36... | collective-permute-start | bytes 3538952 | tf_op jit(solution)/shard_map/ppermute | solution.py:112
  121.5 0.1 pad_add_fusion.place
  121.5 0.0 collective-permute-done.3
  121.5 0.0 collective-permute-done
  121.5 0.0 collective-permute-done.5
  121.5 2.5 %collective-permute-done.2 = bf16[32,48,384]{2,1,0:T(8,128)(2,1)} collective-permute-done((bf16[32,48,384]{2,1,0:T(8,128)(2,1)S(1)}, bf16[32,48,384]{2,1,0:T(8,128)(2,1)}, u32[]{:S(2)}, u32[]{:S(2)}) %collective-permute-start.2) | collective-permute-done | bytes 1179680 | tf_op jit(solution)/shard_map/ppermute | solution.py:112
  124.1 26.4 %contract.1 = bf16[1536,4,384]{2,1,0:T(4,128)(2,1)} custom-call(s32[2]{0:T(128)S(1)} %pad_add_fusion.place, bf16[1536,384]{1,0:T(8,128)(2,1)S(1)} %bitcast.15, bf16[1536,384]{1,0:T(8,128)(2,1)} %bitcast.4.refs_1_, bf16[1536,384]{1,0:T(8,128)(2,1)S(1)} %bitcast.16, bf16[1536,384]{1,0:T(8,128)(2,1)} %bitcast.6.refs_3_, bf16[1536,384]{1,0:T(8,128)(2,1)S(1)} %bitcast.14, ...), custom_call_target="tpu_custom_call" | custom-call | flops 14495514624 | bytes 25165824 | tf_op jit(solution)/shard_map/contract/pallas_call | solution.py:72
  (4 shorter events, 0.0 us)
Async XLA Ops:
  6.5 117.5 %all-gather.3.cloned.1.call-start = ((), (), s32[]{:S(2)}) async-start(), calls=%async_computation.2 | async-start | bytes 10027008 | tf_op jit(solution)/shard_map/all_gather | solution.py:104
  7.6 8.3 %collective-permute-start.6 = (bf16[2,48,1536]{2,1,0:T(8,128)(2,1)S(1)}, bf16[2,48,1536]{2,1,0:T(8,128)(2,1)S(1)}, u32[]{:S(2)}, u32[]{:S(2)}) collective-permute-start(bf16[2,48,1536]{2,1,0:T(8,128)(2,1)S(1)} %reshape.41), channel_id=1, source_target_pairs={{0,1},{1,0},{2,3},{3,2},{4,5},{5,4},{6,7},{7,6},{8,9},{9,8},{10,11... | collective-permute-start | bytes 884744 | tf_op jit(solution)/shard_map/ppermute | solution.py:101
  16.0 1.9 %copy-start = (bf16[2,1,1536,384]{3,2,1,0:T(8,128)(2,1)S(1)}, bf16[2,1,1536,384]{3,2,1,0:T(8,128)(2,1)}, u32[]{:S(2)}) copy-start(bf16[2,1,1536,384]{3,2,1,0:T(8,128)(2,1)} %param.2) | copy-start | bytes 7077892
  48.3 21.8 %all-to-all-start = ((bf16[32,48,384]{2,1,0:T(8,128)(2,1)}), bf16[32,48,384]{2,1,0:T(8,128)(2,1)S(1)}, u32[]{:S(2)}, u32[]{:S(2)}) async-start(bf16[32,48,384]{2,1,0:T(8,128)(2,1)} %bitcast.2), calls=%async_computation | async-start | bytes 2359296 | tf_op jit(solution)/shard_map/all_to_all | solution.py:110
  54.2 37.9 %collective-permute-start.4 = (bf16[32,48,384]{2,1,0:T(8,128)(2,1)S(1)}, bf16[32,48,384]{2,1,0:T(8,128)(2,1)}, u32[]{:S(2)}, u32[]{:S(2)}) collective-permute-start(bf16[32,48,384]{2,1,0:T(8,128)(2,1)S(1)} %all_to_all.10), channel_id=1, source_target_pairs={{0,64},{64,0},{1,65},{65,1},{2,66},{66,2},{3,67},{67,3},{4,68},{68... | collective-permute-start | bytes 3538952 | tf_op jit(solution)/shard_map/ppermute | solution.py:111
  70.2 47.1 %collective-permute-start.1 = (bf16[32,48,384]{2,1,0:T(8,128)(2,1)S(1)}, bf16[32,48,384]{2,1,0:T(8,128)(2,1)S(1)}, u32[]{:S(2)}, u32[]{:S(2)}) collective-permute-start(bf16[32,48,384]{2,1,0:T(8,128)(2,1)S(1)} %all-to-all-done), channel_id=1, source_target_pairs={{0,64},{64,0},{1,65},{65,1},{2,66},{66,2},{3,67},{67,3},{4,68},{68... | collective-permute-start | bytes 3538952 | tf_op jit(solution)/shard_map/ppermute | solution.py:111
  72.6 48.9 %collective-permute-start.3 = (bf16[32,48,384]{2,1,0:T(8,128)(2,1)S(1)}, bf16[32,48,384]{2,1,0:T(8,128)(2,1)}, u32[]{:S(2)}, u32[]{:S(2)}) collective-permute-start(bf16[32,48,384]{2,1,0:T(8,128)(2,1)S(1)} %all_to_all.10), channel_id=1, source_target_pairs={{0,32},{32,0},{1,33},{33,1},{2,34},{34,2},{3,35},{35,3},{4,36},{36... | collective-permute-start | bytes 3538952 | tf_op jit(solution)/shard_map/ppermute | solution.py:112
  81.3 40.3 %collective-permute-start = (bf16[32,48,384]{2,1,0:T(8,128)(2,1)S(1)}, bf16[32,48,384]{2,1,0:T(8,128)(2,1)}, u32[]{:S(2)}, u32[]{:S(2)}) collective-permute-start(bf16[32,48,384]{2,1,0:T(8,128)(2,1)S(1)} %all-to-all-done), channel_id=1, source_target_pairs={{0,32},{32,0},{1,33},{33,1},{2,34},{34,2},{3,35},{35,3},{4,36},{36... | collective-permute-start | bytes 3538952 | tf_op jit(solution)/shard_map/ppermute | solution.py:112
  92.0 29.5 %collective-permute-start.5 = (bf16[32,48,384]{2,1,0:T(8,128)(2,1)}, bf16[32,48,384]{2,1,0:T(8,128)(2,1)}, u32[]{:S(2)}, u32[]{:S(2)}) collective-permute-start(bf16[32,48,384]{2,1,0:T(8,128)(2,1)} %collective-permute-done.4), channel_id=1, source_target_pairs={{0,32},{32,0},{1,33},{33,1},{2,34},{34,2},{3,35},{35,3},{4,36},{36... | collective-permute-start | bytes 3538952 | tf_op jit(solution)/shard_map/ppermute | solution.py:112
  117.2 6.9 %collective-permute-start.2 = (bf16[32,48,384]{2,1,0:T(8,128)(2,1)S(1)}, bf16[32,48,384]{2,1,0:T(8,128)(2,1)}, u32[]{:S(2)}, u32[]{:S(2)}) collective-permute-start(bf16[32,48,384]{2,1,0:T(8,128)(2,1)S(1)} %collective-permute-done.1), channel_id=1, source_target_pairs={{0,32},{32,0},{1,33},{33,1},{2,34},{34,2},{3,35},{35,3},{4,36},{36... | collective-permute-start | bytes 3538952 | tf_op jit(solution)/shard_map/ppermute | solution.py:112
Sparse Core Ops, SparseCore 0:
  17.0 93.1 all-gather.2

commit v3 on v2

v3 whole, which is shorter than its diff:
```python
import jax
import jax.numpy as jnp
from jax import lax
from jax.experimental import pallas as pl
from jax.experimental.pallas import tpu as pltpu
from jax.sharding import Mesh, PartitionSpec as P

FINE = ("xh", "core", "z", "y", "xl")
ROW = ("z", "y", "xl")
SWAP = [(0, 1), (1, 0)]
UP = [(n, (n + 1) % 4) for n in range(4)]
DOWN = [(n, (n - 1) % 4) for n in range(4)]
ACROSS = [(n, (n + 2) % 4) for n in range(4)]
TILE = 384
OFFSETS = (0, 3, 1, 2)


def contract_kernel(place, *refs):
    blocks, gathered, (out, lhs, mat, total, staged, lsem, wsem, osem) = refs[:8], refs[8:18], refs[18:]
    rows, qa = blocks[0].shape
    nk, qc = out.shape[1:]
    xh, core, z0, y0 = place[0], place[1], place[2], place[3]
    steps = [(i, far) for far in (0, 1) for i in (0, 1)]

    def planes(i):
        own, low, high, first, last = gathered[5 * i : 5 * i + 5]
        for offset, ref in zip(OFFSETS, (own, low, high)):
            yield offset, [(n, ref, n) for n in range(4)]
        yield OFFSETS[3], [(n, (first, last)[n // 2], n % 2) for n in range(4)]

    def start_matrix(s):
        i, far = steps[s]
        slot = s % 2
        half = 1 - xh if far else xh
        for outer, inner in planes(i):
            for n, ref, index in inner:
                if i == 0:
                    z, y = lax.rem(z0 + outer, 4), lax.rem(y0 + OFFSETS[n], 4)
                else:
                    z, y = lax.rem(z0 + OFFSETS[n], 4), lax.rem(y0 + outer, 4)

                @pl.when(z // 2 == half)
                def _(z=z, y=y, ref=ref, index=index):
                    pltpu.make_async_copy(
                        ref.at[index], mat.at[slot, lax.rem(z, 2), y], wsem.at[slot]
                    ).start()

    def wait_matrix(s):
        pltpu.make_async_copy(mat.at[s % 2], mat.at[s % 2], wsem.at[s % 2]).wait()

    def lhs_copies(s):
        i, far = steps[s]
        slot = s % 2
        mine, other = blocks[4 * i + 2 * far], blocks[4 * i + 2 * far + 1]
        first = pl.multiple_of(core * qa, 128)
        second = pl.multiple_of((1 - core) * qa, 128)
        return (
            pltpu.make_async_copy(mine, lhs.at[slot, :, pl.ds(first, qa)], lsem.at[slot, 0]),
            pltpu.make_async_copy(other, lhs.at[slot, :, pl.ds(second, qa)], lsem.at[slot, 1]),
        )

    def start(s):
        start_matrix(s)
        for c in lhs_copies(s):
            c.start()

    start(0)
    stores = []
    for s in range(len(steps)):
        if s + 1 < len(steps):
            start(s + 1)
        wait_matrix(s)
        for c in lhs_copies(s):
            c.wait()
        slot = s % 2
        matrix = mat[slot].reshape(2 * qa, nk * qc)
        for m in range(rows // TILE):
            at = pl.ds(m * TILE, TILE)
            term = jnp.dot(lhs[slot, at, :], matrix, preferred_element_type=jnp.float32)
            if s:
                term = term + total[at, :]
            if s + 1 < len(steps):
                total[at, :] = term
            else:
                staged[at] = term.astype(staged.dtype).reshape(TILE, nk, qc)
                stores.append(pltpu.make_async_copy(staged.at[at], out.at[at], osem.at[m]))
                stores[-1].start()
    for c in stores:
        c.wait()


def contract(place, blocks, gathered, nk, qc):
    rows, qa = blocks[0].shape
    any_space = pl.BlockSpec(memory_space=pl.ANY)
    return pl.pallas_call(
        contract_kernel,
        out_shape=jax.ShapeDtypeStruct((rows, nk, qc), jnp.bfloat16),
        in_specs=[pl.BlockSpec(memory_space=pltpu.SMEM)] + [any_space] * 18,
        out_specs=any_space,
        scratch_shapes=[
            pltpu.VMEM((2, rows, 2 * qa), jnp.bfloat16),
            pltpu.VMEM((2, 2, 4) + gathered[0].shape[1:], jnp.bfloat16),
            pltpu.VMEM((rows, nk * qc), jnp.float32),
            pltpu.VMEM((rows, nk, qc), jnp.bfloat16),
            pltpu.SemaphoreType.DMA((2, 2)),
            pltpu.SemaphoreType.DMA((2,)),
            pltpu.SemaphoreType.DMA((rows // TILE,)),
        ],
        compiler_params=pltpu.CompilerParams(vmem_limit_bytes=48 << 20),
        cost_estimate=pl.CostEstimate(
            flops=2 * rows * 8 * qa * nk * qc, bytes_accessed=24 << 20, transcendentals=0
        ),
        name="contract",
    )(place, *blocks, *gathered)


def inner_ring(block, axis):
    moved = [lax.ppermute(block, axis, way) for way in (UP, DOWN, ACROSS)]
    return jnp.concatenate([block] + moved, axis=0)


def outer_ring(held, axis):
    return lax.ppermute(held, axis, UP), lax.ppermute(held, axis, DOWN)


def opposite(low, high, axis):
    return lax.ppermute(low[:2], axis, UP), lax.ppermute(high[2:], axis, DOWN)


def on_device(amplitudes, coupling):
    ni, _, v, qa = amplitudes.shape
    rows = lax.axis_size(ROW)
    nb = v // rows
    na, nk, qc = coupling.shape[1:]
    tie = lax.optimization_barrier

    def to_owners(i):
        chunks = amplitudes[i, 0].reshape(rows, nb, qa)
        return lax.all_to_all(chunks, ROW, split_axis=0, concat_axis=0, tiled=True)

    def cross(block):
        return lax.ppermute(block, "xh", SWAP)

    def beside(block):
        return lax.ppermute(block, "core", SWAP)

    mine = coupling.reshape(ni, na, nk * qc)
    other = lax.ppermute(mine, "xl", SWAP)
    lower = lax.axis_index("xl") == 0
    pair = jnp.concatenate([jnp.where(lower, mine, other), jnp.where(lower, other, mine)], axis=1)
    own0 = to_owners(0)
    w0 = inner_ring(pair[0][None], "y")
    w1 = inner_ring(pair[1][None], "z")
    own0, w0, w1, amplitudes = tie((own0, w0, w1, amplitudes))

    far0 = cross(own0)
    own1 = to_owners(1)
    low0, high0 = outer_ring(w0, "z")
    low1, high1 = outer_ring(w1, "y")
    own1, far0 = tie((own1, far0))

    far1 = cross(own1)
    opp0 = opposite(low0, high0, "z")
    opp1 = opposite(low1, high1, "y")
    opp0, opp1, own0, own1, far0 = tie((opp0, opp1, own0, own1, far0))

    own0c, own1c, far0c = beside(own0), beside(own1), beside(far0)
    far1, own0c, own1c, far0c = tie((far1, own0c, own1c, far0c))
    far1c = beside(far1)

    blocks = (own0, own0c, far0, far0c, own1, own1c, far1, far1c)
    blocks = [b.reshape(rows * nb, qa) for b in blocks]
    place = jnp.stack([lax.axis_index(a) for a in ("xh", "core", "z", "y")]).astype(jnp.int32)
    gathered = (w0, low0, high0) + opp0 + (w1, low1, high1) + opp1
    return contract(place, blocks, gathered, nk, qc).reshape(rows, nb, nk, qc)


def solution(mesh):
    fine = Mesh(mesh.devices.reshape(2, 2, 4, 4, 2), FINE)
    placed = P(None, ROW, None, ("xh", "core"))
    return jax.shard_map(
        on_device, mesh=fine, in_specs=(placed, placed), out_specs=placed, check_vma=False
    )
```

time: 158 us -> 150 us (0.949)
  blocking collectives: 29.3 us -> 0 us
  local copies, waits for them, and re-layouts: 3.24 us -> 19.3 us
  starting transfers between devices: 34 us -> 47.6 us
  between operations: 13.4 us -> 0.26 us
  waiting for transfers between devices: 50 us -> 59.2 us
  Pallas kernels: 26.4 us -> 20.8 us
    all_to_all x1 -> x0, blocking collectives: 29.3 us -> none  [on_device(): got = lax.all_to_all(chunks, ROW, split_axis=0, concat_axis=0, tiled=True)]
    ppermute x6 -> x20, waiting for transfers between devices: 30.3 us -> 51.5 us  [the longest x6 20.1 us: inner_ring(): moved = [lax.ppermute(block, axis, way) for way in (UP, DOWN, ACROSS)]]
    slice x1 -> x6, local copies, waits for them, and re-layouts: 1.25 us -> 11.4 us  [the longest x4 6.62 us: opposite(): return (lax.ppermute(low[:2], axis, UP), lax.ppermute(high[2:], axis, DOWN))]
    all_to_all x1 -> x2, starting transfers between devices: 5.82 us -> 14 us  [to_owners(): return lax.all_to_all(chunks, ROW, split_axis=0, concat_axis=0, tiled=True)]
    ppermute x1, waiting for transfers between devices: 6.22 us -> 0.01 us  [on_device(): other = lax.ppermute(mine, 'xl', SWAP)]
    unnamed x2 -> x14, local copies, waits for them, and re-layouts: 0.92 us -> 6.82 us
    all_to_all x1 -> x2, waiting for transfers between devices: 13.4 us -> 7.7 us  [to_owners(): return lax.all_to_all(chunks, ROW, split_axis=0, concat_axis=0, tiled=True)]
    pallas_call x1, Pallas kernels: 26.4 us -> 20.8 us  [contract(): pl.pallas_call(contract_kernel, out_shape=jax.ShapeDtypeStruct((rows, nk,...]
  transfers between devices with their start and end apart: 9 -> 23, of which waited for: 5 -> 10; matrix products, arithmetic and copies ran while one was open for 1% -> 9% of each run, Pallas kernels for 0% -> 0%
where the time goes in v3:
time: 150 us
  waiting for transfers between devices  59.2 us (39%)
  starting transfers between devices  47.6 us (32%)
  Pallas kernels  20.8 us (14%)
  local copies, waits for them, and re-layouts  19.3 us (13%)
  other arithmetic  2.54 us (2%)
    pallas_call x1, Pallas kernels, contract(): pl.pallas_call(contract_kernel, out_shape=jax.ShapeDtypeStruct((rows, nk,...  20.8 us
    ppermute x6, waiting for transfers between devices, inner_ring(): moved = [lax.ppermute(block, axis, way) for way in (UP, DOWN, ACROSS)]  20.1 us
    all_to_all x2, starting transfers between devices, to_owners(): return lax.all_to_all(chunks, ROW, split_axis=0, concat_axis=0, tiled=True)  14 us
    ppermute x2, waiting for transfers between devices, cross(): return lax.ppermute(block, 'xh', SWAP)  11.9 us
    ppermute x4, waiting for transfers between devices, outer_ring(): return (lax.ppermute(held, axis, UP), lax.ppermute(held, axis, DOWN))  10.5 us
    ppermute x4, starting transfers between devices, beside(): return lax.ppermute(block, 'core', SWAP)  9.1 us
    ppermute x6, starting transfers between devices, inner_ring(): moved = [lax.ppermute(block, axis, way) for way in (UP, DOWN, ACROSS)]  9.04 us
    all_to_all x2, waiting for transfers between devices, to_owners(): return lax.all_to_all(chunks, ROW, split_axis=0, concat_axis=0, tiled=True)  7.7 us
  transfers between devices with their start and end apart: 23, of which 10 were waited for; matrix products, arithmetic and copies ran while one was open for 9% of the time, Pallas kernels for 0%

profile of v3, /device:TPU:1, one launch (start us, length us, event | category | flops | bytes accessed | tf_op | source)
XLA Modules:
  0.0 149.7 jit_solution(9587485459122710987)
XLA Ops:
  1.1 2.1 %collective-permute-start = (bf16[2,48,1536]{2,1,0:T(8,128)(2,1)S(1)}, bf16[2,48,1536]{2,1,0:T(8,128)(2,1)S(1)}, u32[]{:S(2)}, u32[]{:S(2)}) collective-permute-start(bf16[2,48,1536]{2,1,0:T(8,128)(2,1)S(1)} %reshape.30), channel_id=1, source_target_pairs={{0,1},{1,0},{2,3},{3,2},{4,5},{5,4},{6,7},{7,6},{8,9},{9,8},{10,11... | collective-permute-start | bytes 884744 | tf_op jit(solution)/shard_map/ppermute | solution.py:148
  3.2 2.4 %slice.24 = bf16[1,1,1536,384]{3,2,1,0:T(8,128)(2,1)} slice(bf16[2,1,1536,384]{3,2,1,0:T(8,128)(2,1)} %param.2), slice={[0:1], [0:1], [0:1536], [0:384]} | slice | bytes 2359296 | tf_op jit(solution)/shard_map/slice | solution.py:138
  5.6 8.1 %all-to-all-start = ((bf16[32,48,384]{2,1,0:T(8,128)(2,1)}), bf16[32,48,384]{2,1,0:T(8,128)(2,1)S(1)}, u32[]{:S(2)}, u32[]{:S(2)}) async-start(bf16[32,48,384]{2,1,0:T(8,128)(2,1)} %bitcast.4), calls=%async_computation | async-start | bytes 2359296 | tf_op jit(solution)/shard_map/all_to_all | solution.py:139
  13.8 2.8 %collective-permute-start.6 = (bf16[1,96,1536]{2,1,0:T(8,128)(2,1)S(1)}, bf16[1,96,1536]{2,1,0:T(8,128)(2,1)S(1)}, u32[]{:S(2)}, u32[]{:S(2)}) collective-permute-start(bf16[1,96,1536]{2,1,0:T(8,128)(2,1)S(1)} %get-tuple-element.39), channel_id=1, source_target_pairs={{0,16},{8,24},{16,0},{24,8},{1,17},{9,25},{17,1},{25,9},{2,18},{10... | collective-permute-start | bytes 884744 | tf_op jit(solution)/shard_map/ppermute | solution.py:118
  18.1 2.7 %collective-permute-start.3 = (bf16[1,96,1536]{2,1,0:T(8,128)(2,1)S(1)}, bf16[1,96,1536]{2,1,0:T(8,128)(2,1)S(1)}, u32[]{:S(2)}, u32[]{:S(2)}) collective-permute-start(bf16[1,96,1536]{2,1,0:T(8,128)(2,1)S(1)} %get-tuple-element.40), channel_id=1, source_target_pairs={{0,4},{2,6},{4,0},{6,2},{1,5},{3,7},{5,1},{7,3},{8,12},{10,14},{12... | collective-permute-start | bytes 884744 | tf_op jit(solution)/shard_map/ppermute | solution.py:118
  21.6 14.2 %collective-permute-done.6 = bf16[1,96,1536]{2,1,0:T(8,128)(2,1)S(1)} collective-permute-done((bf16[1,96,1536]{2,1,0:T(8,128)(2,1)S(1)}, bf16[1,96,1536]{2,1,0:T(8,128)(2,1)S(1)}, u32[]{:S(2)}, u32[]{:S(2)}) %collective-permute-start.6) | collective-permute-done | bytes 294944 | tf_op jit(solution)/shard_map/ppermute | solution.py:118
  37.0 4.3 %collective-permute-done.5 = bf16[1,96,1536]{2,1,0:T(8,128)(2,1)S(1)} collective-permute-done((bf16[1,96,1536]{2,1,0:T(8,128)(2,1)S(1)}, bf16[1,96,1536]{2,1,0:T(8,128)(2,1)S(1)}, u32[]{:S(2)}, u32[]{:S(2)}) %collective-permute-start.5) | collective-permute-done | bytes 294944 | tf_op jit(solution)/shard_map/ppermute | solution.py:118
  46.8 2.5 %collective-permute-start.13 = (bf16[4,96,1536]{2,1,0:T(8,128)(2,1)}, bf16[4,96,1536]{2,1,0:T(8,128)(2,1)}, u32[]{:S(2)}, u32[]{:S(2)}) collective-permute-start(bf16[4,96,1536]{2,1,0:T(8,128)(2,1)} %pad_maximum_fusion.1.refs_13_), channel_id=1, source_target_pairs={{0,6},{2,0},{4,2},{6,4},{1,7},{3,1},{5,3},{7,5},{8,14},{10,8},{12,... | collective-permute-start | bytes 3538952 | tf_op jit(solution)/shard_map/ppermute | solution.py:123
  49.3 2.7 %collective-permute-start.15 = (bf16[32,48,384]{2,1,0:T(8,128)(2,1)S(1)}, bf16[32,48,384]{2,1,0:T(8,128)(2,1)S(1)}, u32[]{:S(2)}, u32[]{:S(2)}) collective-permute-start(bf16[32,48,384]{2,1,0:T(8,128)(2,1)S(1)} %all-to-all-done), channel_id=1, source_target_pairs={{0,64},{64,0},{1,65},{65,1},{2,66},{66,2},{3,67},{67,3},{4,68},{68... | collective-permute-start | bytes 3538952 | tf_op jit(solution)/shard_map/ppermute | solution.py:142
  52.0 2.4 %slice.31 = bf16[1,1,1536,384]{3,2,1,0:T(8,128)(2,1)} slice(bf16[2,1,1536,384]{3,2,1,0:T(8,128)(2,1)} %param.2), slice={[1:2], [0:1], [0:1536], [0:384]} | slice | bytes 2359296 | tf_op jit(solution)/shard_map/slice | solution.py:138
  54.4 5.9 %all-to-all-start.1 = ((bf16[32,48,384]{2,1,0:T(8,128)(2,1)}), bf16[32,48,384]{2,1,0:T(8,128)(2,1)}, u32[]{:S(2)}, u32[]{:S(2)}) async-start(bf16[32,48,384]{2,1,0:T(8,128)(2,1)} %bitcast.5), calls=%async_computation.1 | async-start | bytes 2359296 | tf_op jit(solution)/shard_map/all_to_all | solution.py:139
  60.4 10.5 %collective-permute-done.9.refs_10_ = bf16[4,96,1536]{2,1,0:T(8,128)(2,1)S(1)} collective-permute-done((bf16[4,96,1536]{2,1,0:T(8,128)(2,1)}, bf16[4,96,1536]{2,1,0:T(8,128)(2,1)S(1)}, u32[]{:S(2)}, u32[]{:S(2)}) %collective-permute-start.9) | collective-permute-done | bytes 1179680 | tf_op jit(solution)/shard_map/ppermute | solution.py:123
  72.7 1.7 %collective-permute-start.10 = (bf16[2,96,1536]{2,1,0:T(8,128)(2,1)}, bf16[2,96,1536]{2,1,0:T(8,128)(2,1)S(1)}, u32[]{:S(2)}, u32[]{:S(2)}) collective-permute-start(bf16[2,96,1536]{2,1,0:T(8,128)(2,1)} %slice.35), channel_id=1, source_target_pairs={{0,24},{8,0},{16,8},{24,16},{1,25},{9,1},{17,9},{25,17},{2,26},{10... | collective-permute-start | bytes 1769480 | tf_op jit(solution)/shard_map/ppermute | solution.py:127
  74.4 1.9 %slice.34 = bf16[2,96,1536]{2,1,0:T(8,128)(2,1)} slice(bf16[4,96,1536]{2,1,0:T(8,128)(2,1)} %collective-permute-done.7.refs_9_), slice={[0:2], [0:96], [0:1536]} | slice | bytes 1179648 | tf_op jit(solution)/shard_map/slice | solution.py:127
  76.3 1.9 %slice.37 = bf16[2,96,1536]{2,1,0:T(8,128)(2,1)} slice(bf16[4,96,1536]{2,1,0:T(8,128)(2,1)} %collective-permute-done.13.refs_15_), slice={[2:4], [0:96], [0:1536]} | slice | bytes 1179648 | tf_op jit(solution)/shard_map/slice | solution.py:127
  78.2 3.6 %collective-permute-start.14 = (bf16[2,96,1536]{2,1,0:T(8,128)(2,1)}, bf16[2,96,1536]{2,1,0:T(8,128)(2,1)}, u32[]{:S(2)}, u32[]{:S(2)}) collective-permute-start(bf16[2,96,1536]{2,1,0:T(8,128)(2,1)} %slice.37), channel_id=1, source_target_pairs={{0,6},{2,0},{4,2},{6,4},{1,7},{3,1},{5,3},{7,5},{8,14},{10,8},{12,... | collective-permute-start | bytes 1769480 | tf_op jit(solution)/shard_map/ppermute | solution.py:127
  81.8 1.9 %slice.36 = bf16[2,96,1536]{2,1,0:T(8,128)(2,1)} slice(bf16[4,96,1536]{2,1,0:T(8,128)(2,1)} %collective-permute-done.11.refs_14_), slice={[0:2], [0:96], [0:1536]} | slice | bytes 1179648 | tf_op jit(solution)/shard_map/slice | solution.py:127
  83.8 7.7 %all-to-all-done.1 = bf16[32,48,384]{2,1,0:T(8,128)(2,1)} async-done(((bf16[32,48,384]{2,1,0:T(8,128)(2,1)}), bf16[32,48,384]{2,1,0:T(8,128)(2,1)}, u32[]{:S(2)}, u32[]{:S(2)}) %all-to-all-start.1) | async-done | bytes 1179680 | tf_op jit(solution)/shard_map/all_to_all | solution.py:139
  92.8 4.0 %collective-permute-done.10.refs_12_ = bf16[2,96,1536]{2,1,0:T(8,128)(2,1)S(1)} collective-permute-done((bf16[2,96,1536]{2,1,0:T(8,128)(2,1)}, bf16[2,96,1536]{2,1,0:T(8,128)(2,1)S(1)}, u32[]{:S(2)}, u32[]{:S(2)}) %collective-permute-start.10) | collective-permute-done | bytes 589856 | tf_op jit(solution)/shard_map/ppermute | solution.py:127
  100.6 3.9 %collective-permute-start.17 = (bf16[32,48,384]{2,1,0:T(8,128)(2,1)S(1)}, bf16[32,48,384]{2,1,0:T(8,128)(2,1)S(1)}, u32[]{:S(2)}, u32[]{:S(2)}) collective-permute-start(bf16[32,48,384]{2,1,0:T(8,128)(2,1)S(1)} %all-to-all-done), channel_id=1, source_target_pairs={{0,32},{32,0},{1,33},{33,1},{2,34},{34,2},{3,35},{35,3},{4,36},{36... | collective-permute-start | bytes 3538952 | tf_op jit(solution)/shard_map/ppermute | solution.py:145
  105.0 11.9 %collective-permute-done.16 = bf16[32,48,384]{2,1,0:T(8,128)(2,1)} collective-permute-done((bf16[32,48,384]{2,1,0:T(8,128)(2,1)}, bf16[32,48,384]{2,1,0:T(8,128)(2,1)}, u32[]{:S(2)}, u32[]{:S(2)}) %collective-permute-start.16) | collective-permute-done | bytes 1179680 | tf_op jit(solution)/shard_map/ppermute | solution.py:142
  119.0 4.7 %collective-permute-start.20 = (bf16[32,48,384]{2,1,0:T(8,128)(2,1)}, bf16[32,48,384]{2,1,0:T(8,128)(2,1)}, u32[]{:S(2)}, u32[]{:S(2)}) collective-permute-start(bf16[32,48,384]{2,1,0:T(8,128)(2,1)} %collective-permute-done.16), channel_id=1, source_target_pairs={{0,32},{32,0},{1,33},{33,1},{2,34},{34,2},{3,35},{35,3},{4,36},{36... | collective-permute-start | bytes 3538952 | tf_op jit(solution)/shard_map/ppermute | solution.py:145
  123.8 2.7 %collective-permute-done.20 = bf16[32,48,384]{2,1,0:T(8,128)(2,1)} collective-permute-done((bf16[32,48,384]{2,1,0:T(8,128)(2,1)}, bf16[32,48,384]{2,1,0:T(8,128)(2,1)}, u32[]{:S(2)}, u32[]{:S(2)}) %collective-permute-start.20) | collective-permute-done | bytes 1179680 | tf_op jit(solution)/shard_map/ppermute | solution.py:145
  128.7 20.8 %contract.1 = bf16[1536,4,384]{2,1,0:T(4,128)(2,1)} custom-call(s32[4]{0:T(128)S(1)} %pad_add_fusion.place, bf16[1536,384]{1,0:T(8,128)(2,1)S(1)} %bitcast.15, bf16[1536,384]{1,0:T(8,128)(2,1)S(1)} %bitcast.17, bf16[1536,384]{1,0:T(8,128)(2,1)S(1)} %bitcast.16, bf16[1536,384]{1,0:T(8,128)(2,1)} %bitcast.19, bf16[1536,384]{1,0:T(8,128)(2,1)} %bitcast.10.refs_4_, ...), custom_call_target="tpu_custom_call" | custom-call | flops 14495514624 | bytes 25165824 | tf_op jit(solution)/shard_map/contract/pallas_call | solution.py:95
  (49 shorter events, 22.0 us)
Async XLA Ops:
  1.1 12.6 %collective-permute-start = (bf16[2,48,1536]{2,1,0:T(8,128)(2,1)S(1)}, bf16[2,48,1536]{2,1,0:T(8,128)(2,1)S(1)}, u32[]{:S(2)}, u32[]{:S(2)}) collective-permute-start(bf16[2,48,1536]{2,1,0:T(8,128)(2,1)S(1)} %reshape.30), channel_id=1, source_target_pairs={{0,1},{1,0},{2,3},{3,2},{4,5},{5,4},{6,7},{7,6},{8,9},{9,8},{10,11... | collective-permute-start | bytes 884744 | tf_op jit(solution)/shard_map/ppermute | solution.py:148
  5.6 39.7 %all-to-all-start = ((bf16[32,48,384]{2,1,0:T(8,128)(2,1)}), bf16[32,48,384]{2,1,0:T(8,128)(2,1)S(1)}, u32[]{:S(2)}, u32[]{:S(2)}) async-start(bf16[32,48,384]{2,1,0:T(8,128)(2,1)} %bitcast.4), calls=%async_computation | async-start | bytes 2359296 | tf_op jit(solution)/shard_map/all_to_all | solution.py:139
  13.8 22.0 %collective-permute-start.6 = (bf16[1,96,1536]{2,1,0:T(8,128)(2,1)S(1)}, bf16[1,96,1536]{2,1,0:T(8,128)(2,1)S(1)}, u32[]{:S(2)}, u32[]{:S(2)}) collective-permute-start(bf16[1,96,1536]{2,1,0:T(8,128)(2,1)S(1)} %get-tuple-element.39), channel_id=1, source_target_pairs={{0,16},{8,24},{16,0},{24,8},{1,17},{9,25},{17,1},{25,9},{2,18},{10... | collective-permute-start | bytes 884744 | tf_op jit(solution)/shard_map/ppermute | solution.py:118
  16.6 24.7 %collective-permute-start.5 = (bf16[1,96,1536]{2,1,0:T(8,128)(2,1)S(1)}, bf16[1,96,1536]{2,1,0:T(8,128)(2,1)S(1)}, u32[]{:S(2)}, u32[]{:S(2)}) collective-permute-start(bf16[1,96,1536]{2,1,0:T(8,128)(2,1)S(1)} %get-tuple-element.39), channel_id=1, source_target_pairs={{0,24},{8,0},{16,8},{24,16},{1,25},{9,1},{17,9},{25,17},{2,26},{10... | collective-permute-start | bytes 884744 | tf_op jit(solution)/shard_map/ppermute | solution.py:118
  17.5 25.5 %collective-permute-start.4 = (bf16[1,96,1536]{2,1,0:T(8,128)(2,1)S(1)}, bf16[1,96,1536]{2,1,0:T(8,128)(2,1)S(1)}, u32[]{:S(2)}, u32[]{:S(2)}) collective-permute-start(bf16[1,96,1536]{2,1,0:T(8,128)(2,1)S(1)} %get-tuple-element.39), channel_id=1, source_target_pairs={{0,8},{8,16},{16,24},{24,0},{1,9},{9,17},{17,25},{25,1},{2,10},{10... | collective-permute-start | bytes 884744 | tf_op jit(solution)/shard_map/ppermute | solution.py:118
  18.1 26.1 %collective-permute-start.3 = (bf16[1,96,1536]{2,1,0:T(8,128)(2,1)S(1)}, bf16[1,96,1536]{2,1,0:T(8,128)(2,1)S(1)}, u32[]{:S(2)}, u32[]{:S(2)}) collective-permute-start(bf16[1,96,1536]{2,1,0:T(8,128)(2,1)S(1)} %get-tuple-element.40), channel_id=1, source_target_pairs={{0,4},{2,6},{4,0},{6,2},{1,5},{3,7},{5,1},{7,3},{8,12},{10,14},{12... | collective-permute-start | bytes 884744 | tf_op jit(solution)/shard_map/ppermute | solution.py:118
  20.8 23.4 %collective-permute-start.2 = (bf16[1,96,1536]{2,1,0:T(8,128)(2,1)S(1)}, bf16[1,96,1536]{2,1,0:T(8,128)(2,1)S(1)}, u32[]{:S(2)}, u32[]{:S(2)}) collective-permute-start(bf16[1,96,1536]{2,1,0:T(8,128)(2,1)S(1)} %get-tuple-element.40), channel_id=1, source_target_pairs={{0,6},{2,0},{4,2},{6,4},{1,7},{3,1},{5,3},{7,5},{8,14},{10,8},{12,... | collective-permute-start | bytes 884744 | tf_op jit(solution)/shard_map/ppermute | solution.py:118
  35.8 8.3 %collective-permute-start.1 = (bf16[1,96,1536]{2,1,0:T(8,128)(2,1)S(1)}, bf16[1,96,1536]{2,1,0:T(8,128)(2,1)S(1)}, u32[]{:S(2)}, u32[]{:S(2)}) collective-permute-start(bf16[1,96,1536]{2,1,0:T(8,128)(2,1)S(1)} %get-tuple-element.40), channel_id=1, source_target_pairs={{0,2},{2,4},{4,6},{6,0},{1,3},{3,5},{5,7},{7,1},{8,10},{10,12},{12... | collective-permute-start | bytes 884744 | tf_op jit(solution)/shard_map/ppermute | solution.py:118
  45.3 25.5 %collective-permute-start.9 = (bf16[4,96,1536]{2,1,0:T(8,128)(2,1)}, bf16[4,96,1536]{2,1,0:T(8,128)(2,1)S(1)}, u32[]{:S(2)}, u32[]{:S(2)}) collective-permute-start(bf16[4,96,1536]{2,1,0:T(8,128)(2,1)} %pad_maximum_fusion.refs_8_), channel_id=1, source_target_pairs={{0,24},{8,0},{16,8},{24,16},{1,25},{9,1},{17,9},{25,17},{2,26},{10... | collective-permute-start | bytes 3538952 | tf_op jit(solution)/shard_map/ppermute | solution.py:123
  46.3 28.0 %collective-permute-start.7 = (bf16[4,96,1536]{2,1,0:T(8,128)(2,1)}, bf16[4,96,1536]{2,1,0:T(8,128)(2,1)}, u32[]{:S(2)}, u32[]{:S(2)}) collective-permute-start(bf16[4,96,1536]{2,1,0:T(8,128)(2,1)} %pad_maximum_fusion.refs_8_), channel_id=1, source_target_pairs={{0,8},{8,16},{16,24},{24,0},{1,9},{9,17},{17,25},{25,1},{2,10},{10... | collective-permute-start | bytes 3538952 | tf_op jit(solution)/shard_map/ppermute | solution.py:123
  46.8 29.5 %collective-permute-start.13 = (bf16[4,96,1536]{2,1,0:T(8,128)(2,1)}, bf16[4,96,1536]{2,1,0:T(8,128)(2,1)}, u32[]{:S(2)}, u32[]{:S(2)}) collective-permute-start(bf16[4,96,1536]{2,1,0:T(8,128)(2,1)} %pad_maximum_fusion.1.refs_13_), channel_id=1, source_target_pairs={{0,6},{2,0},{4,2},{6,4},{1,7},{3,1},{5,3},{7,5},{8,14},{10,8},{12,... | collective-permute-start | bytes 3538952 | tf_op jit(solution)/shard_map/ppermute | solution.py:123
  49.3 32.5 %collective-permute-start.11 = (bf16[4,96,1536]{2,1,0:T(8,128)(2,1)}, bf16[4,96,1536]{2,1,0:T(8,128)(2,1)}, u32[]{:S(2)}, u32[]{:S(2)}) collective-permute-start(bf16[4,96,1536]{2,1,0:T(8,128)(2,1)} %pad_maximum_fusion.1.refs_13_), channel_id=1, source_target_pairs={{0,2},{2,4},{4,6},{6,0},{1,3},{3,5},{5,7},{7,1},{8,10},{10,12},{12... | collective-permute-start | bytes 3538952 | tf_op jit(solution)/shard_map/ppermute | solution.py:123
  49.3 42.1 %collective-permute-start.15 = (bf16[32,48,384]{2,1,0:T(8,128)(2,1)S(1)}, bf16[32,48,384]{2,1,0:T(8,128)(2,1)S(1)}, u32[]{:S(2)}, u32[]{:S(2)}) collective-permute-start(bf16[32,48,384]{2,1,0:T(8,128)(2,1)S(1)} %all-to-all-done), channel_id=1, source_target_pairs={{0,64},{64,0},{1,65},{65,1},{2,66},{66,2},{3,67},{67,3},{4,68},{68... | collective-permute-start | bytes 3538952 | tf_op jit(solution)/shard_map/ppermute | solution.py:142
  54.4 37.0 %all-to-all-start.1 = ((bf16[32,48,384]{2,1,0:T(8,128)(2,1)}), bf16[32,48,384]{2,1,0:T(8,128)(2,1)}, u32[]{:S(2)}, u32[]{:S(2)}) async-start(bf16[32,48,384]{2,1,0:T(8,128)(2,1)} %bitcast.5), calls=%async_computation.1 | async-start | bytes 2359296 | tf_op jit(solution)/shard_map/all_to_all | solution.py:139
  72.7 24.1 %collective-permute-start.10 = (bf16[2,96,1536]{2,1,0:T(8,128)(2,1)}, bf16[2,96,1536]{2,1,0:T(8,128)(2,1)S(1)}, u32[]{:S(2)}, u32[]{:S(2)}) collective-permute-start(bf16[2,96,1536]{2,1,0:T(8,128)(2,1)} %slice.35), channel_id=1, source_target_pairs={{0,24},{8,0},{16,8},{24,16},{1,25},{9,1},{17,9},{25,17},{2,26},{10... | collective-permute-start | bytes 1769480 | tf_op jit(solution)/shard_map/ppermute | solution.py:127
  76.3 23.0 %collective-permute-start.8 = (bf16[2,96,1536]{2,1,0:T(8,128)(2,1)}, bf16[2,96,1536]{2,1,0:T(8,128)(2,1)S(1)}, u32[]{:S(2)}, u32[]{:S(2)}) collective-permute-start(bf16[2,96,1536]{2,1,0:T(8,128)(2,1)} %slice.34), channel_id=1, source_target_pairs={{0,8},{8,16},{16,24},{24,0},{1,9},{9,17},{17,25},{25,1},{2,10},{10... | collective-permute-start | bytes 1769480 | tf_op jit(solution)/shard_map/ppermute | solution.py:127
  78.2 21.8 %collective-permute-start.14 = (bf16[2,96,1536]{2,1,0:T(8,128)(2,1)}, bf16[2,96,1536]{2,1,0:T(8,128)(2,1)}, u32[]{:S(2)}, u32[]{:S(2)}) collective-permute-start(bf16[2,96,1536]{2,1,0:T(8,128)(2,1)} %slice.37), channel_id=1, source_target_pairs={{0,6},{2,0},{4,2},{6,4},{1,7},{3,1},{5,3},{7,5},{8,14},{10,8},{12,... | collective-permute-start | bytes 1769480 | tf_op jit(solution)/shard_map/ppermute | solution.py:127
  83.8 16.9 %collective-permute-start.12 = (bf16[2,96,1536]{2,1,0:T(8,128)(2,1)}, bf16[2,96,1536]{2,1,0:T(8,128)(2,1)}, u32[]{:S(2)}, u32[]{:S(2)}) collective-permute-start(bf16[2,96,1536]{2,1,0:T(8,128)(2,1)} %slice.36), channel_id=1, source_target_pairs={{0,2},{2,4},{4,6},{6,0},{1,3},{3,5},{5,7},{7,1},{8,10},{10,12},{12... | collective-permute-start | bytes 1769480 | tf_op jit(solution)/shard_map/ppermute | solution.py:127
  91.5 25.5 %collective-permute-start.16 = (bf16[32,48,384]{2,1,0:T(8,128)(2,1)}, bf16[32,48,384]{2,1,0:T(8,128)(2,1)}, u32[]{:S(2)}, u32[]{:S(2)}) collective-permute-start(bf16[32,48,384]{2,1,0:T(8,128)(2,1)} %all-to-all-done.1), channel_id=1, source_target_pairs={{0,64},{64,0},{1,65},{65,1},{2,66},{66,2},{3,67},{67,3},{4,68},{68... | collective-permute-start | bytes 3538952 | tf_op jit(solution)/shard_map/ppermute | solution.py:142
  100.6 16.3 %collective-permute-start.17 = (bf16[32,48,384]{2,1,0:T(8,128)(2,1)S(1)}, bf16[32,48,384]{2,1,0:T(8,128)(2,1)S(1)}, u32[]{:S(2)}, u32[]{:S(2)}) collective-permute-start(bf16[32,48,384]{2,1,0:T(8,128)(2,1)S(1)} %all-to-all-done), channel_id=1, source_target_pairs={{0,32},{32,0},{1,33},{33,1},{2,34},{34,2},{3,35},{35,3},{4,36},{36... | collective-permute-start | bytes 3538952 | tf_op jit(solution)/shard_map/ppermute | solution.py:145
  104.5 12.5 %collective-permute-start.18 = (bf16[32,48,384]{2,1,0:T(8,128)(2,1)}, bf16[32,48,384]{2,1,0:T(8,128)(2,1)S(1)}, u32[]{:S(2)}, u32[]{:S(2)}) collective-permute-start(bf16[32,48,384]{2,1,0:T(8,128)(2,1)} %all-to-all-done.1), channel_id=1, source_target_pairs={{0,32},{32,0},{1,33},{33,1},{2,34},{34,2},{3,35},{35,3},{4,36},{36... | collective-permute-start | bytes 3538952 | tf_op jit(solution)/shard_map/ppermute | solution.py:145
  104.5 12.5 %collective-permute-start.19 = (bf16[32,48,384]{2,1,0:T(8,128)(2,1)S(1)}, bf16[32,48,384]{2,1,0:T(8,128)(2,1)S(1)}, u32[]{:S(2)}, u32[]{:S(2)}) collective-permute-start(bf16[32,48,384]{2,1,0:T(8,128)(2,1)S(1)} %collective-permute-done.15), channel_id=1, source_target_pairs={{0,32},{32,0},{1,33},{33,1},{2,34},{34,2},{3,35},{35,3},{4,36},{36... | collective-permute-start | bytes 3538952 | tf_op jit(solution)/shard_map/ppermute | solution.py:145
  119.0 7.5 %collective-permute-start.20 = (bf16[32,48,384]{2,1,0:T(8,128)(2,1)}, bf16[32,48,384]{2,1,0:T(8,128)(2,1)}, u32[]{:S(2)}, u32[]{:S(2)}) collective-permute-start(bf16[32,48,384]{2,1,0:T(8,128)(2,1)} %collective-permute-done.16), channel_id=1, source_target_pairs={{0,32},{32,0},{1,33},{33,1},{2,34},{34,2},{3,35},{35,3},{4,36},{36... | collective-permute-start | bytes 3538952 | tf_op jit(solution)/shard_map/ppermute | solution.py:145
  126.5 1.1 copy-start.1
  (6 other events, 5.8 us)

commit v4 on v3

v4 whole, which is shorter than its diff:
```python
import jax
import jax.numpy as jnp
from jax import lax
from jax.experimental import pallas as pl
from jax.experimental.pallas import tpu as pltpu
from jax.sharding import Mesh, PartitionSpec as P

FINE = ("xh", "core", "z", "y", "xl")
ROW = ("z", "y", "xl")
SWAP = [(0, 1), (1, 0)]
UP = [(n, (n + 1) % 4) for n in range(4)]
DOWN = [(n, (n - 1) % 4) for n in range(4)]
ACROSS = [(n, (n + 2) % 4) for n in range(4)]
TILE = 384
OFFSETS = (0, 3, 1, 2)
COSTS = (15, 0.2, 0.2, 7, 0.5)
ANY = pl.BlockSpec(memory_space=pl.ANY)
tie = lax.optimization_barrier


def planes(gathered):
    own, low, high, first, last = gathered
    for offset, ref in zip(OFFSETS, (own, low, high)):
        yield offset, [(n, ref, n) for n in range(4)]
    yield OFFSETS[3], [(n, (first, last)[n // 2], n % 2) for n in range(4)]


def contract_kernel(place, *refs):
    left, gathered, refs = (refs[:4], refs[4:6]), (refs[6:11], refs[11:16]), refs[17:]
    out, lhs, mat, total, staged, lsem, wsem, osem = refs
    nb, qa = left[0][0].shape[2:]
    width = total.shape[1]
    tiles = total.shape[0] // TILE
    per_tile = TILE // (2 * nb)
    core, z0, y0, xh = place[0], place[1], place[2], place[3]
    steps = [(i, half) for i in range(2) for half in range(2)]

    def start_matrix(s):
        i, half = steps[s]
        slot = s % 2
        for outer, inner in planes(gathered[i]):
            for n, ref, index in inner:
                if i == 0:
                    z, y = lax.rem(z0 + outer, 4), lax.rem(y0 + OFFSETS[n], 4)
                else:
                    z, y = lax.rem(z0 + OFFSETS[n], 4), lax.rem(y0 + outer, 4)

                @pl.when(z // 2 == half)
                def _(z=z, y=y, ref=ref, index=index):
                    pltpu.make_async_copy(
                        ref.at[index], mat.at[slot, lax.rem(z, 2), y], wsem.at[slot]
                    ).start()

    def start_left(s):
        i, half = steps[s]
        slot = s % 2
        for n, c in enumerate((core, 1 - core)):
            lanes = pl.ds(pl.multiple_of(c * qa, 128), qa)
            if i == 1:
                for xl in range(2):
                    pltpu.make_async_copy(
                        left[1][n].at[2 * half + xl], lhs.at[slot, :, xl, :, lanes], lsem.at[slot]
                    ).start()
                continue
            for ref, here in ((left[0][n], xh), (left[0][2 + n], 1 - xh)):

                @pl.when(here == half)
                def _(ref=ref, lanes=lanes):
                    pltpu.make_async_copy(ref, lhs.at[slot, :, :, :, lanes], lsem.at[slot]).start()

    def wait(buffer, sem, slot):
        pltpu.make_async_copy(buffer.at[slot], buffer.at[slot], sem.at[slot]).wait()

    start_matrix(0)
    start_left(0)
    stores = []
    for s in range(len(steps)):
        slot = s % 2
        if s + 1 < len(steps):
            start_matrix(s + 1)
            start_left(s + 1)
        wait(mat, wsem, slot)
        wait(lhs, lsem, slot)
        matrix = mat[slot].reshape(2 * qa, width)
        for m in range(tiles):
            at = pl.ds(m * TILE, TILE)
            rows = lhs[slot, m * per_tile : (m + 1) * per_tile].reshape(TILE, 2 * qa)
            term = jnp.dot(rows, matrix, preferred_element_type=jnp.float32)
            if s:
                term = term + total[at, :]
            if s + 1 < len(steps):
                total[at, :] = term
                continue
            staged[at] = term.astype(staged.dtype).reshape((TILE,) + staged.shape[1:])
            stores.append(pltpu.make_async_copy(staged.at[at], out.at[at], osem.at[m]))
            stores[-1].start()
    for c in stores:
        c.wait()


def contract(place, left, gathered, nk, after):
    n_zy = lax.axis_size(("z", "y"))
    nb, qa = left[0].shape[2:]
    rows, width = 2 * n_zy * nb, gathered[0].shape[2]
    dma = pltpu.SemaphoreType.DMA
    shape = jax.ShapeDtypeStruct((rows, nk, width // nk), jnp.bfloat16)
    return pl.pallas_call(
        contract_kernel,
        out_shape=shape,
        in_specs=[pl.BlockSpec(memory_space=pltpu.SMEM)] + [ANY] * 17,
        out_specs=ANY,
        scratch_shapes=[
            pltpu.VMEM((2, n_zy, 2, nb, 2 * qa), jnp.bfloat16),
            pltpu.VMEM((2, 2, 4) + gathered[0].shape[1:], jnp.bfloat16),
            pltpu.VMEM((rows, width), jnp.float32),
            pltpu.VMEM(shape.shape, shape.dtype),
            dma((2,)),
            dma((2,)),
            dma((rows // TILE,)),
        ],
        compiler_params=pltpu.CompilerParams(vmem_limit_bytes=40 << 20),
        cost_estimate=pl.CostEstimate(
            flops=2 * rows * 8 * qa * width, bytes_accessed=24 << 20, transcendentals=0
        ),
        name="contract",
    )(place, *left, *gathered, after)


def order(token, us, vmem=1):
    def body(t, o):
        o[...] = t[...]

    return pl.pallas_call(
        body,
        out_shape=jax.ShapeDtypeStruct(token.shape, token.dtype),
        compiler_params=pltpu.CompilerParams(vmem_limit_bytes=vmem << 20),
        cost_estimate=pl.CostEstimate(
            flops=int(us * 1.15e9), bytes_accessed=8192, transcendentals=0
        ),
        name="order",
    )(token)


def inner_ring(block, axis):
    moved = [lax.ppermute(block, axis, way) for way in (UP, DOWN, ACROSS)]
    return jnp.concatenate([block] + moved, axis=0)


def outer_ring(held, axis):
    return lax.ppermute(held, axis, UP), lax.ppermute(held, axis, DOWN)


def opposite(low, high, axis):
    return lax.ppermute(low[:2], axis, UP), lax.ppermute(high[2:], axis, DOWN)


def on_device(amplitudes, coupling):
    ni, _, v, qa = amplitudes.shape
    nb = v // lax.axis_size(ROW)
    n_zy = lax.axis_size(("z", "y"))
    na, nk, qc = coupling.shape[1:]
    token = jnp.zeros((8, 128), jnp.float32) + coupling[0, 0, 0, 0].astype(jnp.float32)

    def exchange(block, axes):
        return lax.all_to_all(block, axes, split_axis=0, concat_axis=0, tiled=True)

    def beside(block):
        return lax.ppermute(block, "core", SWAP)

    mine = coupling.reshape(ni, na, nk * qc)
    other = lax.ppermute(mine, "xl", SWAP)
    own0 = exchange(amplitudes[0, 0].reshape(n_zy * 2, nb, qa), ROW)
    part1 = amplitudes[1, 0].reshape(n_zy, 2, nb, qa)
    lower = lax.axis_index("xl") == 0
    pair = jnp.concatenate([jnp.where(lower, mine, other), jnp.where(lower, other, mine)], axis=1)

    w0 = inner_ring(pair[0][None], "y")
    w1 = inner_ring(pair[1][None], "z")
    token, own0, w0, w1, part1 = tie((token, own0, w0, w1, part1))

    zy1 = exchange(part1, ("z", "y"))
    token = order(token, COSTS[0])
    token, w0, w1, own0 = tie((token, w0, w1, own0))

    low0, high0 = outer_ring(w0, "z")
    low1, high1 = outer_ring(w1, "y")
    far0 = lax.ppermute(own0, "xh", SWAP)
    token = order(token, COSTS[1])
    token, zy1 = tie((token, zy1))
    zy1 = zy1.transpose(1, 0, 2, 3)
    x1 = exchange(jnp.concatenate([zy1, zy1], axis=0), ("xh", "xl"))
    token = order(token, COSTS[2])
    token, low0, high0, low1, high1, far0 = tie((token, low0, high0, low1, high1, far0))

    opp0 = opposite(low0, high0, "z")
    opp1 = opposite(low1, high1, "y")
    far0c = beside(far0)
    token = order(token, COSTS[3], 60)
    token, opp0, opp1, far0c, own0 = tie((token, opp0, opp1, far0c, own0))
    own0c = beside(own0)
    token = order(token, COSTS[4])
    token, x1 = tie((token, x1))
    x1c = beside(x1)

    place = jnp.stack([lax.axis_index(a) for a in ("core", "z", "y", "xh")]).astype(jnp.int32)
    left = tuple(b.reshape(n_zy, 2, nb, qa) for b in (own0, own0c, far0, far0c)) + (x1, x1c)
    gathered = (w0, low0, high0) + opp0 + (w1, low1, high1) + opp1
    return contract(place, left, gathered, nk, token).reshape(2 * n_zy, nb, nk, qc)


def solution(mesh):
    fine = Mesh(mesh.devices.reshape(2, 2, 4, 4, 2), FINE)
    placed = P(None, ROW, None, ("xh", "core"))
    return jax.shard_map(
        on_device, mesh=fine, in_specs=(placed, placed), out_specs=placed, check_vma=False
    )
```

time: 150 us -> 149 us (level)
  waiting for transfers between devices: 59.2 us -> 65.2 us
  starting transfers between devices: 47.6 us -> 42.5 us
  local copies, waits for them, and re-layouts: 19.3 us -> 15.7 us
  Pallas kernels: 20.8 us -> 22.4 us
    ppermute x2 -> x1, waiting for transfers between devices: 11.9 us -> 2.32 us  [on_device(): far0 = lax.ppermute(own0, 'xh', SWAP)]
    ppermute x4, waiting for transfers between devices: 6.17 us -> 13.7 us  [opposite(): return (lax.ppermute(low[:2], axis, UP), lax.ppermute(high[2:], axis, DOWN))]
    ppermute x4 -> x3, starting transfers between devices: 9.1 us -> 2.67 us  [beside(): return lax.ppermute(block, 'core', SWAP)]
    unnamed x14 -> x4, local copies, waits for them, and re-layouts: 6.82 us -> 1.27 us
    ppermute x4, waiting for transfers between devices: 10.5 us -> 15.8 us  [outer_ring(): return (lax.ppermute(held, axis, UP), lax.ppermute(held, axis, DOWN))]
    all_to_all x2 -> x3, starting transfers between devices: 14 us -> 17.6 us  [exchange(): return lax.all_to_all(block, axes, split_axis=0, concat_axis=0, tiled=True)]
    ppermute x4 -> x3, waiting for transfers between devices: 2.75 us -> 6.03 us  [beside(): return lax.ppermute(block, 'core', SWAP)]
    concatenate x2, other arithmetic: 2.38 us -> 0.3 us  [inner_ring(): return jnp.concatenate([block] + moved, axis=0)]
  transfers between devices with their start and end apart: 23 -> 22, of which waited for: 10 -> 12; matrix products, arithmetic and copies ran while one was open for 9% -> 10% of each run, Pallas kernels for 0% -> 1%
where the time goes in v4:
time: 149 us; the launch traced here: 148 us
  waiting for transfers between devices  65.2 us (44%)
  starting transfers between devices  42.5 us (29%)
  Pallas kernels  22.4 us (15%)
  local copies, waits for them, and re-layouts  15.7 us (11%)
  other arithmetic  2.13 us (1%)
    pallas_call x1, Pallas kernels, contract(): pl.pallas_call(contract_kernel, out_shape=shape, in_specs=[pl.BlockSpec(m...  21.1 us
    ppermute x6, waiting for transfers between devices, inner_ring(): moved = [lax.ppermute(block, axis, way) for way in (UP, DOWN, ACROSS)]  18.9 us
    all_to_all x3, starting transfers between devices, exchange(): return lax.all_to_all(block, axes, split_axis=0, concat_axis=0, tiled=True)  17.6 us
    ppermute x4, waiting for transfers between devices, outer_ring(): return (lax.ppermute(held, axis, UP), lax.ppermute(held, axis, DOWN))  15.8 us
    ppermute x4, waiting for transfers between devices, opposite(): return (lax.ppermute(low[:2], axis, UP), lax.ppermute(high[2:], axis, DOWN))  13.7 us
    ppermute x6, starting transfers between devices, inner_ring(): moved = [lax.ppermute(block, axis, way) for way in (UP, DOWN, ACROSS)]  9.04 us
    all_to_all x3, waiting for transfers between devices, exchange(): return lax.all_to_all(block, axes, split_axis=0, concat_axis=0, tiled=True)  8.31 us
    slice x4, local copies, waits for them, and re-layouts, opposite(): return (lax.ppermute(low[:2], axis, UP), lax.ppermute(high[2:], axis, DOWN))  6.92 us
  transfers between devices with their start and end apart: 22, of which 12 were waited for; matrix products, arithmetic and copies ran while one was open for 10% of the time, Pallas kernels for 1%

profile of v4, /device:TPU:1, one launch (start us, length us, event | category | flops | bytes accessed | tf_op | source)
XLA Modules:
  0.0 148.3 jit_solution(448759306180028900)
XLA Ops:
  1.1 2.1 %collective-permute-start = (bf16[2,48,1536]{2,1,0:T(8,128)(2,1)S(1)}, bf16[2,48,1536]{2,1,0:T(8,128)(2,1)S(1)}, u32[]{:S(2)}, u32[]{:S(2)}) collective-permute-start(bf16[2,48,1536]{2,1,0:T(8,128)(2,1)S(1)} %reshape.20), channel_id=1, source_target_pairs={{0,1},{1,0},{2,3},{3,2},{4,5},{5,4},{6,7},{7,6},{8,9},{9,8},{10,11... | collective-permute-start | bytes 884744 | tf_op jit(solution)/shard_map/ppermute | solution.py:171
  3.2 3.3 %fusion.1 = (bf16[1,1,1536,384]{3,2,1,0:T(8,128)(2,1)}, bf16[1,1,1536,384]{3,2,1,0:T(8,128)(2,1)}) fusion(bf16[2,1,1536,384]{3,2,1,0:T(8,128)(2,1)} %param.2), kind=kLoop, calls=%fused_computation.11 | loop fusion | bytes 4718592 | tf_op jit(solution)/shard_map/slice | solution.py:173
  6.5 8.1 %all-to-all-start = ((bf16[32,48,384]{2,1,0:T(8,128)(2,1)}), bf16[32,48,384]{2,1,0:T(8,128)(2,1)S(1)}, u32[]{:S(2)}, u32[]{:S(2)}) async-start(bf16[32,48,384]{2,1,0:T(8,128)(2,1)} %bitcast.5), calls=%async_computation | async-start | bytes 2359296 | tf_op jit(solution)/shard_map/all_to_all | solution.py:165
  14.7 2.8 %collective-permute-start.6 = (bf16[1,96,1536]{2,1,0:T(8,128)(2,1)S(1)}, bf16[1,96,1536]{2,1,0:T(8,128)(2,1)S(1)}, u32[]{:S(2)}, u32[]{:S(2)}) collective-permute-start(bf16[1,96,1536]{2,1,0:T(8,128)(2,1)S(1)} %get-tuple-element.59), channel_id=1, source_target_pairs={{0,16},{8,24},{16,0},{24,8},{1,17},{9,25},{17,1},{25,9},{2,18},{10... | collective-permute-start | bytes 884744 | tf_op jit(solution)/shard_map/ppermute | solution.py:145
  18.9 2.7 %collective-permute-start.3 = (bf16[1,96,1536]{2,1,0:T(8,128)(2,1)S(1)}, bf16[1,96,1536]{2,1,0:T(8,128)(2,1)S(1)}, u32[]{:S(2)}, u32[]{:S(2)}) collective-permute-start(bf16[1,96,1536]{2,1,0:T(8,128)(2,1)S(1)} %get-tuple-element.60), channel_id=1, source_target_pairs={{0,4},{2,6},{4,0},{6,2},{1,5},{3,7},{5,1},{7,3},{8,12},{10,14},{12... | collective-permute-start | bytes 884744 | tf_op jit(solution)/shard_map/ppermute | solution.py:145
  22.5 14.2 %collective-permute-done.6 = bf16[1,96,1536]{2,1,0:T(8,128)(2,1)S(1)} collective-permute-done((bf16[1,96,1536]{2,1,0:T(8,128)(2,1)S(1)}, bf16[1,96,1536]{2,1,0:T(8,128)(2,1)S(1)}, u32[]{:S(2)}, u32[]{:S(2)}) %collective-permute-start.6) | collective-permute-done | bytes 294944 | tf_op jit(solution)/shard_map/ppermute | solution.py:145
  39.1 3.1 %collective-permute-done.5 = bf16[1,96,1536]{2,1,0:T(8,128)(2,1)S(1)} collective-permute-done((bf16[1,96,1536]{2,1,0:T(8,128)(2,1)S(1)}, bf16[1,96,1536]{2,1,0:T(8,128)(2,1)S(1)}, u32[]{:S(2)}, u32[]{:S(2)}) %collective-permute-start.5) | collective-permute-done | bytes 294944 | tf_op jit(solution)/shard_map/ppermute | solution.py:145
  44.8 5.1 %all-to-all-start.1 = ((bf16[16,2,48,384]{3,2,1,0:T(8,128)(2,1)}), bf16[16,2,48,384]{3,2,1,0:T(8,128)(2,1)}, u32[]{:S(2)}, u32[]{:S(2)}) async-start(bf16[16,2,48,384]{3,2,1,0:T(8,128)(2,1)} %bitcast.18), calls=%async_computation.1 | async-start | bytes 2359296 | tf_op jit(solution)/shard_map/all_to_all | solution.py:165
  49.9 2.8 %collective-permute-start.11 = (bf16[32,48,384]{2,1,0:T(8,128)(2,1)S(1)}, bf16[32,48,384]{2,1,0:T(8,128)(2,1)}, u32[]{:S(2)}, u32[]{:S(2)}) collective-permute-start(bf16[32,48,384]{2,1,0:T(8,128)(2,1)S(1)} %all-to-all-done), channel_id=1, source_target_pairs={{0,64},{64,0},{1,65},{65,1},{2,66},{66,2},{3,67},{67,3},{4,68},{68... | collective-permute-start | bytes 3538952 | tf_op jit(solution)/shard_map/ppermute | solution.py:187
  52.7 2.5 %collective-permute-start.8 = (bf16[4,96,1536]{2,1,0:T(8,128)(2,1)S(1)}, bf16[4,96,1536]{2,1,0:T(8,128)(2,1)}, u32[]{:S(2)}, u32[]{:S(2)}) collective-permute-start(bf16[4,96,1536]{2,1,0:T(8,128)(2,1)S(1)} %pad_maximum_fusion.1.refs_6_), channel_id=1, source_target_pairs={{0,24},{8,0},{16,8},{24,16},{1,25},{9,1},{17,9},{25,17},{2,26},{10... | collective-permute-start | bytes 3538952 | tf_op jit(solution)/shard_map/ppermute | solution.py:150
  55.2 2.4 %collective-permute-start.10 = (bf16[4,96,1536]{2,1,0:T(8,128)(2,1)S(1)}, bf16[4,96,1536]{2,1,0:T(8,128)(2,1)}, u32[]{:S(2)}, u32[]{:S(2)}) collective-permute-start(bf16[4,96,1536]{2,1,0:T(8,128)(2,1)S(1)} %pad_maximum_fusion.2.refs_11_), channel_id=1, source_target_pairs={{0,6},{2,0},{4,2},{6,4},{1,7},{3,1},{5,3},{7,5},{8,14},{10,8},{12,... | collective-permute-start | bytes 3538952 | tf_op jit(solution)/shard_map/ppermute | solution.py:150
  57.6 8.3 %all-to-all-done.1 = bf16[16,2,48,384]{3,2,1,0:T(8,128)(2,1)} async-done(((bf16[16,2,48,384]{3,2,1,0:T(8,128)(2,1)}), bf16[16,2,48,384]{3,2,1,0:T(8,128)(2,1)}, u32[]{:S(2)}, u32[]{:S(2)}) %all-to-all-start.1) | async-done | bytes 1179680 | tf_op jit(solution)/shard_map/all_to_all | solution.py:165
  69.0 4.5 %all-to-all-start.2 = ((bf16[4,16,48,384]{3,2,1,0:T(8,128)(2,1)}), bf16[4,16,48,384]{3,2,1,0:T(8,128)(2,1)}, u32[]{:S(2)}, u32[]{:S(2)}) async-start(bf16[4,16,48,384]{3,2,1,0:T(8,128)(2,1)} %pad_maximum_fusion), calls=%async_computation.2 | async-start | bytes 4718592 | tf_op jit(solution)/shard_map/all_to_all | solution.py:165
  74.1 2.3 %collective-permute-done.11 = bf16[32,48,384]{2,1,0:T(8,128)(2,1)} collective-permute-done((bf16[32,48,384]{2,1,0:T(8,128)(2,1)S(1)}, bf16[32,48,384]{2,1,0:T(8,128)(2,1)}, u32[]{:S(2)}, u32[]{:S(2)}) %collective-permute-start.11) | collective-permute-done | bytes 1179680 | tf_op jit(solution)/shard_map/ppermute | solution.py:187
  76.5 13.6 %collective-permute-done.8.refs_8_ = bf16[4,96,1536]{2,1,0:T(8,128)(2,1)} collective-permute-done((bf16[4,96,1536]{2,1,0:T(8,128)(2,1)S(1)}, bf16[4,96,1536]{2,1,0:T(8,128)(2,1)}, u32[]{:S(2)}, u32[]{:S(2)}) %collective-permute-start.8) | collective-permute-done | bytes 1179680 | tf_op jit(solution)/shard_map/ppermute | solution.py:150
  90.0 2.3 %collective-permute-done.7.refs_7_ = bf16[4,96,1536]{2,1,0:T(8,128)(2,1)} collective-permute-done((bf16[4,96,1536]{2,1,0:T(8,128)(2,1)S(1)}, bf16[4,96,1536]{2,1,0:T(8,128)(2,1)}, u32[]{:S(2)}, u32[]{:S(2)}) %collective-permute-start.7) | collective-permute-done | bytes 1179680 | tf_op jit(solution)/shard_map/ppermute | solution.py:150
  94.2 1.9 %slice.33 = bf16[2,96,1536]{2,1,0:T(8,128)(2,1)} slice(bf16[4,96,1536]{2,1,0:T(8,128)(2,1)} %collective-permute-done.8.refs_8_), slice={[2:4], [0:96], [0:1536]} | slice | bytes 1179648 | tf_op jit(solution)/shard_map/slice | solution.py:154
  96.2 2.0 %slice.34 = bf16[2,96,1536]{2,1,0:T(8,128)(2,1)} slice(bf16[4,96,1536]{2,1,0:T(8,128)(2,1)} %collective-permute-done.9.refs_12_), slice={[0:2], [0:96], [0:1536]} | slice | bytes 1179648 | tf_op jit(solution)/shard_map/slice | solution.py:154
  98.1 1.9 %slice.35 = bf16[2,96,1536]{2,1,0:T(8,128)(2,1)} slice(bf16[4,96,1536]{2,1,0:T(8,128)(2,1)} %collective-permute-done.10.refs_13_), slice={[2:4], [0:96], [0:1536]} | slice | bytes 1179648 | tf_op jit(solution)/shard_map/slice | solution.py:154
  100.1 1.9 %collective-permute-start.15 = (bf16[2,96,1536]{2,1,0:T(8,128)(2,1)}, bf16[2,96,1536]{2,1,0:T(8,128)(2,1)}, u32[]{:S(2)}, u32[]{:S(2)}) collective-permute-start(bf16[2,96,1536]{2,1,0:T(8,128)(2,1)} %slice.35), channel_id=1, source_target_pairs={{0,6},{2,0},{4,2},{6,4},{1,7},{3,1},{5,3},{7,5},{8,14},{10,8},{12,... | collective-permute-start | bytes 1769480 | tf_op jit(solution)/shard_map/ppermute | solution.py:154
  104.7 10.7 %collective-permute-done.15.refs_15_ = bf16[2,96,1536]{2,1,0:T(8,128)(2,1)} collective-permute-done((bf16[2,96,1536]{2,1,0:T(8,128)(2,1)}, bf16[2,96,1536]{2,1,0:T(8,128)(2,1)}, u32[]{:S(2)}, u32[]{:S(2)}) %collective-permute-start.15) | collective-permute-done | bytes 589856 | tf_op jit(solution)/shard_map/ppermute | solution.py:154
  115.3 2.8 %collective-permute-done.14.refs_14_ = bf16[2,96,1536]{2,1,0:T(8,128)(2,1)} collective-permute-done((bf16[2,96,1536]{2,1,0:T(8,128)(2,1)}, bf16[2,96,1536]{2,1,0:T(8,128)(2,1)}, u32[]{:S(2)}, u32[]{:S(2)}) %collective-permute-start.14) | collective-permute-done | bytes 589856 | tf_op jit(solution)/shard_map/ppermute | solution.py:154
  121.0 5.7 %collective-permute-done.17 = bf16[32,48,384]{2,1,0:T(8,128)(2,1)} collective-permute-done((bf16[32,48,384]{2,1,0:T(8,128)(2,1)S(1)}, bf16[32,48,384]{2,1,0:T(8,128)(2,1)}, u32[]{:S(2)}, u32[]{:S(2)}) %collective-permute-start.17) | collective-permute-done | bytes 1179680 | tf_op jit(solution)/shard_map/ppermute | solution.py:168
  127.0 21.1 %contract.1 = bf16[1536,4,384]{2,1,0:T(4,128)(2,1)} custom-call(s32[4]{0:T(128)S(1)} %pad_add_fusion.place, bf16[16,2,48,384]{3,2,1,0:T(8,128)(2,1)S(1)} %bitcast.16, bf16[16,2,48,384]{3,2,1,0:T(8,128)(2,1)} %bitcast.8.refs_1_, bf16[16,2,48,384]{3,2,1,0:T(8,128)(2,1)} %bitcast.9.refs_2_, bf16[16,2,48,384]{3,2,1,0:T(8,128)(2,1)} %bitcast.10.refs_3_, ...), custom_call_target="tpu_custom_call" | custom-call | flops 14495514624 | bytes 25165824 | tf_op jit(solution)/shard_map/contract/pallas_call | solution.py:107
  (45 shorter events, 20.1 us)
Async XLA Ops:
  1.1 13.5 %collective-permute-start = (bf16[2,48,1536]{2,1,0:T(8,128)(2,1)S(1)}, bf16[2,48,1536]{2,1,0:T(8,128)(2,1)S(1)}, u32[]{:S(2)}, u32[]{:S(2)}) collective-permute-start(bf16[2,48,1536]{2,1,0:T(8,128)(2,1)S(1)} %reshape.20), channel_id=1, source_target_pairs={{0,1},{1,0},{2,3},{3,2},{4,5},{5,4},{6,7},{7,6},{8,9},{9,8},{10,11... | collective-permute-start | bytes 884744 | tf_op jit(solution)/shard_map/ppermute | solution.py:171
  6.5 37.7 %all-to-all-start = ((bf16[32,48,384]{2,1,0:T(8,128)(2,1)}), bf16[32,48,384]{2,1,0:T(8,128)(2,1)S(1)}, u32[]{:S(2)}, u32[]{:S(2)}) async-start(bf16[32,48,384]{2,1,0:T(8,128)(2,1)} %bitcast.5), calls=%async_computation | async-start | bytes 2359296 | tf_op jit(solution)/shard_map/all_to_all | solution.py:165
  14.7 22.0 %collective-permute-start.6 = (bf16[1,96,1536]{2,1,0:T(8,128)(2,1)S(1)}, bf16[1,96,1536]{2,1,0:T(8,128)(2,1)S(1)}, u32[]{:S(2)}, u32[]{:S(2)}) collective-permute-start(bf16[1,96,1536]{2,1,0:T(8,128)(2,1)S(1)} %get-tuple-element.59), channel_id=1, source_target_pairs={{0,16},{8,24},{16,0},{24,8},{1,17},{9,25},{17,1},{25,9},{2,18},{10... | collective-permute-start | bytes 884744 | tf_op jit(solution)/shard_map/ppermute | solution.py:145
  17.5 24.7 %collective-permute-start.5 = (bf16[1,96,1536]{2,1,0:T(8,128)(2,1)S(1)}, bf16[1,96,1536]{2,1,0:T(8,128)(2,1)S(1)}, u32[]{:S(2)}, u32[]{:S(2)}) collective-permute-start(bf16[1,96,1536]{2,1,0:T(8,128)(2,1)S(1)} %get-tuple-element.59), channel_id=1, source_target_pairs={{0,24},{8,0},{16,8},{24,16},{1,25},{9,1},{17,9},{25,17},{2,26},{10... | collective-permute-start | bytes 884744 | tf_op jit(solution)/shard_map/ppermute | solution.py:145
  18.4 25.5 %collective-permute-start.4 = (bf16[1,96,1536]{2,1,0:T(8,128)(2,1)S(1)}, bf16[1,96,1536]{2,1,0:T(8,128)(2,1)S(1)}, u32[]{:S(2)}, u32[]{:S(2)}) collective-permute-start(bf16[1,96,1536]{2,1,0:T(8,128)(2,1)S(1)} %get-tuple-element.59), channel_id=1, source_target_pairs={{0,8},{8,16},{16,24},{24,0},{1,9},{9,17},{17,25},{25,1},{2,10},{10... | collective-permute-start | bytes 884744 | tf_op jit(solution)/shard_map/ppermute | solution.py:145
  18.9 25.0 %collective-permute-start.3 = (bf16[1,96,1536]{2,1,0:T(8,128)(2,1)S(1)}, bf16[1,96,1536]{2,1,0:T(8,128)(2,1)S(1)}, u32[]{:S(2)}, u32[]{:S(2)}) collective-permute-start(bf16[1,96,1536]{2,1,0:T(8,128)(2,1)S(1)} %get-tuple-element.60), channel_id=1, source_target_pairs={{0,4},{2,6},{4,0},{6,2},{1,5},{3,7},{5,1},{7,3},{8,12},{10,14},{12... | collective-permute-start | bytes 884744 | tf_op jit(solution)/shard_map/ppermute | solution.py:145
  21.6 22.3 %collective-permute-start.2 = (bf16[1,96,1536]{2,1,0:T(8,128)(2,1)S(1)}, bf16[1,96,1536]{2,1,0:T(8,128)(2,1)S(1)}, u32[]{:S(2)}, u32[]{:S(2)}) collective-permute-start(bf16[1,96,1536]{2,1,0:T(8,128)(2,1)S(1)} %get-tuple-element.60), channel_id=1, source_target_pairs={{0,6},{2,0},{4,2},{6,4},{1,7},{3,1},{5,3},{7,5},{8,14},{10,8},{12,... | collective-permute-start | bytes 884744 | tf_op jit(solution)/shard_map/ppermute | solution.py:145
  36.7 7.3 %collective-permute-start.1 = (bf16[1,96,1536]{2,1,0:T(8,128)(2,1)S(1)}, bf16[1,96,1536]{2,1,0:T(8,128)(2,1)S(1)}, u32[]{:S(2)}, u32[]{:S(2)}) collective-permute-start(bf16[1,96,1536]{2,1,0:T(8,128)(2,1)S(1)} %get-tuple-element.60), channel_id=1, source_target_pairs={{0,2},{2,4},{4,6},{6,0},{1,3},{3,5},{5,7},{7,1},{8,10},{10,12},{12... | collective-permute-start | bytes 884744 | tf_op jit(solution)/shard_map/ppermute | solution.py:145
  44.8 21.1 %all-to-all-start.1 = ((bf16[16,2,48,384]{3,2,1,0:T(8,128)(2,1)}), bf16[16,2,48,384]{3,2,1,0:T(8,128)(2,1)}, u32[]{:S(2)}, u32[]{:S(2)}) async-start(bf16[16,2,48,384]{3,2,1,0:T(8,128)(2,1)} %bitcast.18), calls=%async_computation.1 | async-start | bytes 2359296 | tf_op jit(solution)/shard_map/all_to_all | solution.py:165
  49.9 26.5 %collective-permute-start.11 = (bf16[32,48,384]{2,1,0:T(8,128)(2,1)S(1)}, bf16[32,48,384]{2,1,0:T(8,128)(2,1)}, u32[]{:S(2)}, u32[]{:S(2)}) collective-permute-start(bf16[32,48,384]{2,1,0:T(8,128)(2,1)S(1)} %all-to-all-done), channel_id=1, source_target_pairs={{0,64},{64,0},{1,65},{65,1},{2,66},{66,2},{3,67},{67,3},{4,68},{68... | collective-permute-start | bytes 3538952 | tf_op jit(solution)/shard_map/ppermute | solution.py:187
  52.7 37.3 %collective-permute-start.8 = (bf16[4,96,1536]{2,1,0:T(8,128)(2,1)S(1)}, bf16[4,96,1536]{2,1,0:T(8,128)(2,1)}, u32[]{:S(2)}, u32[]{:S(2)}) collective-permute-start(bf16[4,96,1536]{2,1,0:T(8,128)(2,1)S(1)} %pad_maximum_fusion.1.refs_6_), channel_id=1, source_target_pairs={{0,24},{8,0},{16,8},{24,16},{1,25},{9,1},{17,9},{25,17},{2,26},{10... | collective-permute-start | bytes 3538952 | tf_op jit(solution)/shard_map/ppermute | solution.py:150
  55.2 37.0 %collective-permute-start.7 = (bf16[4,96,1536]{2,1,0:T(8,128)(2,1)S(1)}, bf16[4,96,1536]{2,1,0:T(8,128)(2,1)}, u32[]{:S(2)}, u32[]{:S(2)}) collective-permute-start(bf16[4,96,1536]{2,1,0:T(8,128)(2,1)S(1)} %pad_maximum_fusion.1.refs_6_), channel_id=1, source_target_pairs={{0,8},{8,16},{16,24},{24,0},{1,9},{9,17},{17,25},{25,1},{2,10},{10... | collective-permute-start | bytes 3538952 | tf_op jit(solution)/shard_map/ppermute | solution.py:150
  55.2 37.0 %collective-permute-start.10 = (bf16[4,96,1536]{2,1,0:T(8,128)(2,1)S(1)}, bf16[4,96,1536]{2,1,0:T(8,128)(2,1)}, u32[]{:S(2)}, u32[]{:S(2)}) collective-permute-start(bf16[4,96,1536]{2,1,0:T(8,128)(2,1)S(1)} %pad_maximum_fusion.2.refs_11_), channel_id=1, source_target_pairs={{0,6},{2,0},{4,2},{6,4},{1,7},{3,1},{5,3},{7,5},{8,14},{10,8},{12,... | collective-permute-start | bytes 3538952 | tf_op jit(solution)/shard_map/ppermute | solution.py:150
  57.6 34.7 %collective-permute-start.9 = (bf16[4,96,1536]{2,1,0:T(8,128)(2,1)S(1)}, bf16[4,96,1536]{2,1,0:T(8,128)(2,1)}, u32[]{:S(2)}, u32[]{:S(2)}) collective-permute-start(bf16[4,96,1536]{2,1,0:T(8,128)(2,1)S(1)} %pad_maximum_fusion.2.refs_11_), channel_id=1, source_target_pairs={{0,2},{2,4},{4,6},{6,0},{1,3},{3,5},{5,7},{7,1},{8,10},{10,12},{12... | collective-permute-start | bytes 3538952 | tf_op jit(solution)/shard_map/ppermute | solution.py:150
  69.0 50.1 %all-to-all-start.2 = ((bf16[4,16,48,384]{3,2,1,0:T(8,128)(2,1)}), bf16[4,16,48,384]{3,2,1,0:T(8,128)(2,1)}, u32[]{:S(2)}, u32[]{:S(2)}) async-start(bf16[4,16,48,384]{3,2,1,0:T(8,128)(2,1)} %pad_maximum_fusion), calls=%async_computation.2 | async-start | bytes 4718592 | tf_op jit(solution)/shard_map/all_to_all | solution.py:165
  73.5 0.6 copy-start
  92.3 26.1 %collective-permute-start.16 = (bf16[32,48,384]{2,1,0:T(8,128)(2,1)}, bf16[32,48,384]{2,1,0:T(8,128)(2,1)}, u32[]{:S(2)}, u32[]{:S(2)}) collective-permute-start(bf16[32,48,384]{2,1,0:T(8,128)(2,1)} %collective-permute-done.11), channel_id=1, source_target_pairs={{0,32},{32,0},{1,33},{33,1},{2,34},{34,2},{3,35},{35,3},{4,36},{36... | collective-permute-start | bytes 3538952 | tf_op jit(solution)/shard_map/ppermute | solution.py:168
  100.1 15.3 %collective-permute-start.15 = (bf16[2,96,1536]{2,1,0:T(8,128)(2,1)}, bf16[2,96,1536]{2,1,0:T(8,128)(2,1)}, u32[]{:S(2)}, u32[]{:S(2)}) collective-permute-start(bf16[2,96,1536]{2,1,0:T(8,128)(2,1)} %slice.35), channel_id=1, source_target_pairs={{0,6},{2,0},{4,2},{6,4},{1,7},{3,1},{5,3},{7,5},{8,14},{10,8},{12,... | collective-permute-start | bytes 1769480 | tf_op jit(solution)/shard_map/ppermute | solution.py:154
  101.9 16.2 %collective-permute-start.14 = (bf16[2,96,1536]{2,1,0:T(8,128)(2,1)}, bf16[2,96,1536]{2,1,0:T(8,128)(2,1)}, u32[]{:S(2)}, u32[]{:S(2)}) collective-permute-start(bf16[2,96,1536]{2,1,0:T(8,128)(2,1)} %slice.34), channel_id=1, source_target_pairs={{0,2},{2,4},{4,6},{6,0},{1,3},{3,5},{5,7},{7,1},{8,10},{10,12},{12... | collective-permute-start | bytes 1769480 | tf_op jit(solution)/shard_map/ppermute | solution.py:154
  101.9 16.2 %collective-permute-start.13 = (bf16[2,96,1536]{2,1,0:T(8,128)(2,1)}, bf16[2,96,1536]{2,1,0:T(8,128)(2,1)}, u32[]{:S(2)}, u32[]{:S(2)}) collective-permute-start(bf16[2,96,1536]{2,1,0:T(8,128)(2,1)} %slice.33), channel_id=1, source_target_pairs={{0,24},{8,0},{16,8},{24,16},{1,25},{9,1},{17,9},{25,17},{2,26},{10... | collective-permute-start | bytes 1769480 | tf_op jit(solution)/shard_map/ppermute | solution.py:154
  103.1 15.3 %collective-permute-start.12 = (bf16[2,96,1536]{2,1,0:T(8,128)(2,1)S(1)}, bf16[2,96,1536]{2,1,0:T(8,128)(2,1)}, u32[]{:S(2)}, u32[]{:S(2)}) collective-permute-start(bf16[2,96,1536]{2,1,0:T(8,128)(2,1)S(1)} %slice.32), channel_id=1, source_target_pairs={{0,8},{8,16},{16,24},{24,0},{1,9},{9,17},{17,25},{25,1},{2,10},{10... | collective-permute-start | bytes 1769480 | tf_op jit(solution)/shard_map/ppermute | solution.py:154
  118.4 0.7 copy-start.1
  119.1 7.9 %collective-permute-start.18 = (bf16[4,16,48,384]{3,2,1,0:T(8,128)(2,1)}, bf16[4,16,48,384]{3,2,1,0:T(8,128)(2,1)}, u32[]{:S(2)}, u32[]{:S(2)}) collective-permute-start(bf16[4,16,48,384]{3,2,1,0:T(8,128)(2,1)} %all-to-all-done.2.refs_4_), channel_id=1, source_target_pairs={{0,32},{32,0},{1,33},{33,1},{2,34},{34,2},{3,35},{35,3},{4,36},{36... | collective-permute-start | bytes 7077896 | tf_op jit(solution)/shard_map/ppermute | solution.py:168
  120.8 5.8 %collective-permute-start.17 = (bf16[32,48,384]{2,1,0:T(8,128)(2,1)S(1)}, bf16[32,48,384]{2,1,0:T(8,128)(2,1)}, u32[]{:S(2)}, u32[]{:S(2)}) collective-permute-start(bf16[32,48,384]{2,1,0:T(8,128)(2,1)S(1)} %all-to-all-done), channel_id=1, source_target_pairs={{0,32},{32,0},{1,33},{33,1},{2,34},{34,2},{3,35},{35,3},{4,36},{36... | collective-permute-start | bytes 3538952 | tf_op jit(solution)/shard_map/ppermute | solution.py:168

commit v5 on v4

v5 whole, which is shorter than its diff:
```python
import functools

import jax
import jax.numpy as jnp
from jax import lax
from jax.experimental import pallas as pl
from jax.experimental.pallas import tpu as pltpu
from jax.sharding import Mesh, PartitionSpec as P

FINE = ("xh", "core", "z", "y", "xl")
ROW = ("z", "y", "xl")
SWAP = [(0, 1), (1, 0)]
UP = [(n, (n + 1) % 4) for n in range(4)]
DOWN = [(n, (n - 1) % 4) for n in range(4)]
ACROSS = [(n, (n + 2) % 4) for n in range(4)]
TILE = 384
OFFSETS = (0, 3, 1, 2)
COSTS = (15, 0.2, 0.2, 0.5, 0.2)
ANY = pl.BlockSpec(memory_space=pl.ANY)
tie = lax.optimization_barrier


def planes(gathered):
    own, low, high, first, last = gathered
    for offset, ref in zip(OFFSETS, (own, low, high)):
        yield offset, [(n, ref, n) for n in range(4)]
    yield OFFSETS[3], [(n, (first, last)[n // 2], n % 2) for n in range(4)]


def contract_kernel(last, place, *refs):
    left0, refs = refs[:4], refs[4:]
    if last:
        left1, across, gathered, so_far, refs = refs[:2], refs[2:4], refs[4:9], refs[9], refs[11:]
        out, lhs, mat, total, staged, lsem, wsem, tsem, osem = refs
        steps = (None, 0, 1)
    else:
        gathered, (out, lhs, mat, total, lsem, wsem, osem) = refs[:3], refs[3:]
        steps = (0, 1)
    nb, qa = left0[0].shape[2:]
    rows, width = total.shape
    tiles = rows // TILE
    per_tile = TILE // (2 * nb)
    core, z0, y0, xh = place[0], place[1], place[2], place[3]
    away = lax.rem(z0 + 2, 4)

    def copy_block(ref, index, slot, z, y):
        pltpu.make_async_copy(ref.at[index], mat.at[slot, z, y], wsem.at[slot, z]).start()

    def start_matrix(s):
        slot = s % 2
        if steps[s] is None:
            for n in range(4):
                copy_block(across[n // 2], n % 2, slot, 0, lax.rem(y0 + OFFSETS[n], 4))
            return
        blocks = (
            planes(gathered)
            if last
            else [(o, [(n, ref, n) for n in range(4)]) for o, ref in zip(OFFSETS, gathered)]
        )
        for outer, inner in blocks:
            for n, ref, index in inner:
                if last:
                    z, y = lax.rem(z0 + OFFSETS[n], 4), lax.rem(y0 + outer, 4)
                else:
                    z, y = lax.rem(z0 + outer, 4), lax.rem(y0 + OFFSETS[n], 4)

                @pl.when(z // 2 == steps[s])
                def _(z=z, y=y, ref=ref, index=index):
                    copy_block(ref, index, slot, lax.rem(z, 2), y)

    def wait_matrix(s):
        slot = s % 2
        for z in range(1 if steps[s] is None else 2):
            part = mat.at[slot, z]
            if last:
                pltpu.make_async_copy(part, part, wsem.at[slot, z]).wait()
                continue
            absent = away == 2 * steps[s] + z

            @pl.when(jnp.logical_not(absent))
            def _(part=part, z=z):
                pltpu.make_async_copy(part, part, wsem.at[slot, z]).wait()

            @pl.when(absent)
            def _(part=part):
                part[...] = jnp.zeros(part.shape, part.dtype)

    def left_part(s):
        return lhs.at[s % 2, :, :, :, :qa] if steps[s] is None else lhs.at[s % 2]

    def start_left(s):
        slot, half = s % 2, steps[s]
        for n, c in enumerate((core, 1 - core)):
            lanes = pl.ds(pl.multiple_of(c * qa, 128), qa)
            if last and half is not None:
                for xl in range(2):
                    pltpu.make_async_copy(
                        left1[n].at[2 * half + xl], lhs.at[slot, :, xl, :, lanes], lsem.at[slot]
                    ).start()
                continue
            for ref, here in ((left0[n], xh), (left0[2 + n], 1 - xh)):
                if half is None:
                    wanted, target = away == 2 * here + c, left_part(s)
                else:
                    wanted, target = here == half, lhs.at[slot, :, :, :, lanes]

                @pl.when(wanted)
                def _(ref=ref, target=target):
                    pltpu.make_async_copy(ref, target, lsem.at[slot]).start()

    def at(m):
        return pl.ds(m * TILE, TILE)

    start_matrix(0)
    start_left(0)
    sums = []
    if last:
        for m in range(tiles):
            sums.append(pltpu.make_async_copy(so_far.at[at(m)], total.at[at(m)], tsem.at[m]))
            sums[-1].start()
    stores = []
    for s in range(len(steps)):
        slot = s % 2
        if s + 1 < len(steps):
            start_matrix(s + 1)
            start_left(s + 1)
        wait_matrix(s)
        pltpu.make_async_copy(left_part(s), left_part(s), lsem.at[slot]).wait()
        depth = qa if steps[s] is None else 2 * qa
        if steps[s] is None:
            matrix = mat[slot, 0].reshape(depth, width)
        else:
            matrix = mat[slot].reshape(depth, width)
        for m in range(tiles):
            some = lhs[slot, m * per_tile : (m + 1) * per_tile, :, :, :depth].reshape(TILE, depth)
            term = jnp.dot(some, matrix, preferred_element_type=jnp.float32)
            if last and s == 0:
                sums[m].wait()
            if last or s:
                term = term + total[at(m), :]
            end = s + 1 == len(steps)
            if last and end:
                staged[at(m)] = term.astype(staged.dtype).reshape((TILE,) + staged.shape[1:])
            else:
                total[at(m), :] = term
            if end:
                source = staged if last else total
                stores.append(pltpu.make_async_copy(source.at[at(m)], out.at[at(m)], osem.at[m]))
                stores[-1].start()
    for c in stores:
        c.wait()


def contract(place, operands, shape, cost):
    last = shape.dtype == jnp.bfloat16
    n_zy = lax.axis_size(("z", "y"))
    nb, qa = operands[0].shape[2:]
    block = operands[4 if not last else 8].shape[1:]
    rows = 2 * n_zy * nb
    dma = pltpu.SemaphoreType.DMA
    scratch = [
        pltpu.VMEM((2, n_zy, 2, nb, 2 * qa), jnp.bfloat16),
        pltpu.VMEM((2, 2, 4) + block, jnp.bfloat16),
        pltpu.VMEM((rows, block[1]), jnp.float32),
    ]
    sems = [dma((2,)), dma((2, 2)), dma((rows // TILE,))]
    if last:
        scratch.append(pltpu.VMEM(shape.shape, shape.dtype))
        sems.append(dma((rows // TILE,)))
    return pl.pallas_call(
        functools.partial(contract_kernel, last),
        out_shape=shape,
        in_specs=[pl.BlockSpec(memory_space=pltpu.SMEM)] + [ANY] * len(operands),
        out_specs=ANY,
        scratch_shapes=scratch + sems,
        compiler_params=pltpu.CompilerParams(vmem_limit_bytes=40 << 20),
        cost_estimate=pl.CostEstimate(
            flops=int(cost * 1.15e9), bytes_accessed=1 << 20, transcendentals=0
        ),
        name="contract_last" if last else "contract_first",
    )(place, *operands)


def order(token, us, vmem=1):
    def body(t, o):
        o[...] = t[...]

    return pl.pallas_call(
        body,
        out_shape=jax.ShapeDtypeStruct(token.shape, token.dtype),
        compiler_params=pltpu.CompilerParams(vmem_limit_bytes=vmem << 20),
        cost_estimate=pl.CostEstimate(
            flops=int(us * 1.15e9), bytes_accessed=8192, transcendentals=0
        ),
        name="order",
    )(token)


def inner_ring(block, axis):
    moved = [lax.ppermute(block, axis, way) for way in (UP, DOWN, ACROSS)]
    return jnp.concatenate([block] + moved, axis=0)


def outer_ring(held, axis):
    return lax.ppermute(held, axis, UP), lax.ppermute(held, axis, DOWN)


def opposite(low, high, axis):
    return lax.ppermute(low[:2], axis, UP), lax.ppermute(high[2:], axis, DOWN)


def on_device(amplitudes, coupling):
    ni, _, v, qa = amplitudes.shape
    nb = v // lax.axis_size(ROW)
    n_zy = lax.axis_size(("z", "y"))
    na, nk, qc = coupling.shape[1:]
    token = jnp.zeros((8, 128), jnp.float32) + coupling[0, 0, 0, 0].astype(jnp.float32)

    def exchange(block, axes):
        return lax.all_to_all(block, axes, split_axis=0, concat_axis=0, tiled=True)

    def beside(block):
        return lax.ppermute(block, "core", SWAP)

    mine = coupling.reshape(ni, na, nk * qc)
    other = lax.ppermute(mine, "xl", SWAP)
    own0 = exchange(amplitudes[0, 0].reshape(n_zy * 2, nb, qa), ROW)
    part1 = amplitudes[1, 0].reshape(n_zy, 2, nb, qa)
    lower = lax.axis_index("xl") == 0
    pair = jnp.concatenate([jnp.where(lower, mine, other), jnp.where(lower, other, mine)], axis=1)

    w0 = inner_ring(pair[0][None], "y")
    w1 = inner_ring(pair[1][None], "z")
    token, own0, w0, w1, part1 = tie((token, own0, w0, w1, part1))

    zy1 = exchange(part1, ("z", "y"))
    token = order(token, COSTS[0])
    token, w0, w1, own0 = tie((token, w0, w1, own0))

    low0, high0 = outer_ring(w0, "z")
    low1, high1 = outer_ring(w1, "y")
    far0 = lax.ppermute(own0, "xh", SWAP)
    token = order(token, COSTS[1])
    token, zy1 = tie((token, zy1))
    zy1 = zy1.transpose(1, 0, 2, 3)
    x1 = exchange(jnp.concatenate([zy1, zy1], axis=0), ("xh", "xl"))
    token = order(token, COSTS[2])
    token, low0, high0, low1, high1, far0 = tie((token, low0, high0, low1, high1, far0))

    opp0 = opposite(low0, high0, "z")
    opp1 = opposite(low1, high1, "y")
    far0c, own0c = beside(far0), beside(own0)
    place = jnp.stack([lax.axis_index(a) for a in ("core", "z", "y", "xh")]).astype(jnp.int32)
    left0 = tuple(b.reshape(n_zy, 2, nb, qa) for b in (own0, own0c, far0, far0c))
    rows = 2 * n_zy * nb
    total = jax.ShapeDtypeStruct((rows, nk * qc), jnp.float32)
    total = contract(place, left0 + (w0, low0, high0), total, COSTS[3])
    token, total, opp0, opp1 = tie((token, total, opp0, opp1))
    token = order(token, COSTS[4], 60)
    token, x1 = tie((token, x1))

    operands = left0 + (x1, beside(x1)) + opp0 + (w1, low1, high1) + opp1 + (total, token)
    result = jax.ShapeDtypeStruct((rows, nk, qc), jnp.bfloat16)
    return contract(place, operands, result, 12).reshape(2 * n_zy, nb, nk, qc)


def solution(mesh):
    fine = Mesh(mesh.devices.reshape(2, 2, 4, 4, 2), FINE)
    placed = P(None, ROW, None, ("xh", "core"))
    return jax.shard_map(
        on_device, mesh=fine, in_specs=(placed, placed), out_specs=placed, check_vma=False
    )
```

time: 149 us -> 152 us (1.020)
  waiting for transfers between devices: 65.2 us -> 50.5 us
  Pallas kernels: 22.4 us -> 31.5 us
  starting transfers between devices: 42.5 us -> 47.1 us
  local copies, waits for them, and re-layouts: 15.7 us -> 18.2 us
    ppermute x4, waiting for transfers between devices: 13.7 us -> 3.18 us  [opposite(): return (lax.ppermute(low[:2], axis, UP), lax.ppermute(high[2:], axis, DOWN))]
    pallas_call x1 -> x2, Pallas kernels: 21.1 us -> 30.2 us  [contract(): pl.pallas_call(functools.partial(contract_kernel, last), out_shape=shape,...]
    ppermute x4, waiting for transfers between devices: 15.8 us -> 10.8 us  [outer_ring(): return (lax.ppermute(held, axis, UP), lax.ppermute(held, axis, DOWN))]
    ppermute x3, starting transfers between devices: 2.67 us -> 7.58 us  [beside(): return lax.ppermute(block, 'core', SWAP)]
    all_to_all x3, waiting for transfers between devices: 8.31 us -> 11.1 us  [exchange(): return lax.all_to_all(block, axes, split_axis=0, concat_axis=0, tiled=True)]
    unnamed x4 -> x8, local copies, waits for them, and re-layouts: 1.27 us -> 3.98 us
    ppermute x3, waiting for transfers between devices: 6.03 us -> 4.38 us  [beside(): return lax.ppermute(block, 'core', SWAP)]
  transfers between devices with their start and end apart: 22 -> 22, of which waited for: 12 -> 11; matrix products, arithmetic and copies ran while one was open for 10% -> 10% of each run, Pallas kernels for 1% -> 9%
where the time goes in v5:
time: 152 us; the launch traced here: 151 us
  waiting for transfers between devices  50.5 us (33%)
  starting transfers between devices  47.1 us (31%)
  Pallas kernels  31.5 us (21%)
  local copies, waits for them, and re-layouts  18.2 us (12%)
  other arithmetic  3.17 us (2%)
    pallas_call x2, Pallas kernels, contract(): pl.pallas_call(functools.partial(contract_kernel, last), out_shape=shape,...  30.2 us
    ppermute x6, waiting for transfers between devices, inner_ring(): moved = [lax.ppermute(block, axis, way) for way in (UP, DOWN, ACROSS)]  18.9 us
    all_to_all x3, starting transfers between devices, exchange(): return lax.all_to_all(block, axes, split_axis=0, concat_axis=0, tiled=True)  17 us
    all_to_all x3, waiting for transfers between devices, exchange(): return lax.all_to_all(block, axes, split_axis=0, concat_axis=0, tiled=True)  11.1 us
    ppermute x4, waiting for transfers between devices, outer_ring(): return (lax.ppermute(held, axis, UP), lax.ppermute(held, axis, DOWN))  10.8 us
    ppermute x6, starting transfers between devices, inner_ring(): moved = [lax.ppermute(block, axis, way) for way in (UP, DOWN, ACROSS)]  9.04 us
    ppermute x3, starting transfers between devices, beside(): return lax.ppermute(block, 'core', SWAP)  7.58 us
    slice x4, local copies, waits for them, and re-layouts, opposite(): return (lax.ppermute(low[:2], axis, UP), lax.ppermute(high[2:], axis, DOWN))  6.64 us
  transfers between devices with their start and end apart: 22, of which 11 were waited for; matrix products, arithmetic and copies ran while one was open for 10% of the time, Pallas kernels for 9%

profile of v5, /device:TPU:1, one launch (start us, length us, event | category | flops | bytes accessed | tf_op | source)
XLA Modules:
  0.0 150.8 jit_solution(6736691400967268581)
XLA Ops:
  1.1 2.1 %collective-permute-start = (bf16[2,48,1536]{2,1,0:T(8,128)(2,1)S(1)}, bf16[2,48,1536]{2,1,0:T(8,128)(2,1)S(1)}, u32[]{:S(2)}, u32[]{:S(2)}) collective-permute-start(bf16[2,48,1536]{2,1,0:T(8,128)(2,1)S(1)} %reshape.20), channel_id=1, source_target_pairs={{0,1},{1,0},{2,3},{3,2},{4,5},{5,4},{6,7},{7,6},{8,9},{9,8},{10,11... | collective-permute-start | bytes 884744 | tf_op jit(solution)/shard_map/ppermute | solution.py:226
  3.2 3.3 %fusion.1 = (bf16[1,1,1536,384]{3,2,1,0:T(8,128)(2,1)}, bf16[1,1,1536,384]{3,2,1,0:T(8,128)(2,1)}) fusion(bf16[2,1,1536,384]{3,2,1,0:T(8,128)(2,1)} %param.2), kind=kLoop, calls=%fused_computation.11 | loop fusion | bytes 4718592 | tf_op jit(solution)/shard_map/slice | solution.py:228
  6.5 8.1 %all-to-all-start = ((bf16[32,48,384]{2,1,0:T(8,128)(2,1)}), bf16[32,48,384]{2,1,0:T(8,128)(2,1)S(1)}, u32[]{:S(2)}, u32[]{:S(2)}) async-start(bf16[32,48,384]{2,1,0:T(8,128)(2,1)} %bitcast.5), calls=%async_computation | async-start | bytes 2359296 | tf_op jit(solution)/shard_map/all_to_all | solution.py:220
  14.7 2.8 %collective-permute-start.6 = (bf16[1,96,1536]{2,1,0:T(8,128)(2,1)S(1)}, bf16[1,96,1536]{2,1,0:T(8,128)(2,1)S(1)}, u32[]{:S(2)}, u32[]{:S(2)}) collective-permute-start(bf16[1,96,1536]{2,1,0:T(8,128)(2,1)S(1)} %get-tuple-element.57), channel_id=1, source_target_pairs={{0,16},{8,24},{16,0},{24,8},{1,17},{9,25},{17,1},{25,9},{2,18},{10... | collective-permute-start | bytes 884744 | tf_op jit(solution)/shard_map/ppermute | solution.py:200
  18.9 2.7 %collective-permute-start.3 = (bf16[1,96,1536]{2,1,0:T(8,128)(2,1)S(1)}, bf16[1,96,1536]{2,1,0:T(8,128)(2,1)S(1)}, u32[]{:S(2)}, u32[]{:S(2)}) collective-permute-start(bf16[1,96,1536]{2,1,0:T(8,128)(2,1)S(1)} %get-tuple-element.58), channel_id=1, source_target_pairs={{0,4},{2,6},{4,0},{6,2},{1,5},{3,7},{5,1},{7,3},{8,12},{10,14},{12... | collective-permute-start | bytes 884744 | tf_op jit(solution)/shard_map/ppermute | solution.py:200
  22.5 14.2 %collective-permute-done.6 = bf16[1,96,1536]{2,1,0:T(8,128)(2,1)S(1)} collective-permute-done((bf16[1,96,1536]{2,1,0:T(8,128)(2,1)S(1)}, bf16[1,96,1536]{2,1,0:T(8,128)(2,1)S(1)}, u32[]{:S(2)}, u32[]{:S(2)}) %collective-permute-start.6) | collective-permute-done | bytes 294944 | tf_op jit(solution)/shard_map/ppermute | solution.py:200
  39.1 3.1 %collective-permute-done.5 = bf16[1,96,1536]{2,1,0:T(8,128)(2,1)S(1)} collective-permute-done((bf16[1,96,1536]{2,1,0:T(8,128)(2,1)S(1)}, bf16[1,96,1536]{2,1,0:T(8,128)(2,1)S(1)}, u32[]{:S(2)}, u32[]{:S(2)}) %collective-permute-start.5) | collective-permute-done | bytes 294944 | tf_op jit(solution)/shard_map/ppermute | solution.py:200
  45.8 2.8 %collective-permute-start.12 = (bf16[32,48,384]{2,1,0:T(8,128)(2,1)S(1)}, bf16[32,48,384]{2,1,0:T(8,128)(2,1)}, u32[]{:S(2)}, u32[]{:S(2)}) collective-permute-start(bf16[32,48,384]{2,1,0:T(8,128)(2,1)S(1)} %all-to-all-done), channel_id=1, source_target_pairs={{0,64},{64,0},{1,65},{65,1},{2,66},{66,2},{3,67},{67,3},{4,68},{68... | collective-permute-start | bytes 3538952 | tf_op jit(solution)/shard_map/ppermute | solution.py:242
  48.6 4.5 %all-to-all-start.1 = ((bf16[16,2,48,384]{3,2,1,0:T(8,128)(2,1)}), bf16[16,2,48,384]{3,2,1,0:T(8,128)(2,1)}, u32[]{:S(2)}, u32[]{:S(2)}) async-start(bf16[16,2,48,384]{3,2,1,0:T(8,128)(2,1)} %bitcast.6), calls=%async_computation.1 | async-start | bytes 2359296 | tf_op jit(solution)/shard_map/all_to_all | solution.py:220
  53.1 2.5 %collective-permute-start.9 = (bf16[4,96,1536]{2,1,0:T(8,128)(2,1)S(1)}, bf16[4,96,1536]{2,1,0:T(8,128)(2,1)S(1)}, u32[]{:S(2)}, u32[]{:S(2)}) collective-permute-start(bf16[4,96,1536]{2,1,0:T(8,128)(2,1)S(1)} %pad_maximum_fusion.1.refs_4_), channel_id=1, source_target_pairs={{0,24},{8,0},{16,8},{24,16},{1,25},{9,1},{17,9},{25,17},{2,26},{10... | collective-permute-start | bytes 3538952 | tf_op jit(solution)/shard_map/ppermute | solution.py:205
  55.7 2.4 %collective-permute-start.11 = (bf16[4,96,1536]{2,1,0:T(8,128)(2,1)}, bf16[4,96,1536]{2,1,0:T(8,128)(2,1)}, u32[]{:S(2)}, u32[]{:S(2)}) collective-permute-start(bf16[4,96,1536]{2,1,0:T(8,128)(2,1)} %pad_maximum_fusion.2.refs_8_), channel_id=1, source_target_pairs={{0,6},{2,0},{4,2},{6,4},{1,7},{3,1},{5,3},{7,5},{8,14},{10,8},{12,... | collective-permute-start | bytes 3538952 | tf_op jit(solution)/shard_map/ppermute | solution.py:205
  58.1 11.1 %all-to-all-done.1 = bf16[16,2,48,384]{3,2,1,0:T(8,128)(2,1)} async-done(((bf16[16,2,48,384]{3,2,1,0:T(8,128)(2,1)}), bf16[16,2,48,384]{3,2,1,0:T(8,128)(2,1)}, u32[]{:S(2)}, u32[]{:S(2)}) %all-to-all-start.1) | async-done | bytes 1179680 | tf_op jit(solution)/shard_map/all_to_all | solution.py:220
  70.6 2.1 %collective-permute-done.12 = bf16[32,48,384]{2,1,0:T(8,128)(2,1)} collective-permute-done((bf16[32,48,384]{2,1,0:T(8,128)(2,1)S(1)}, bf16[32,48,384]{2,1,0:T(8,128)(2,1)}, u32[]{:S(2)}, u32[]{:S(2)}) %collective-permute-start.12) | collective-permute-done | bytes 1179680 | tf_op jit(solution)/shard_map/ppermute | solution.py:242
  72.7 4.4 %collective-permute-start.7 = (bf16[32,48,384]{2,1,0:T(8,128)(2,1)S(1)}, bf16[32,48,384]{2,1,0:T(8,128)(2,1)}, u32[]{:S(2)}, u32[]{:S(2)}) collective-permute-start(bf16[32,48,384]{2,1,0:T(8,128)(2,1)S(1)} %all-to-all-done), channel_id=1, source_target_pairs={{0,32},{32,0},{1,33},{33,1},{2,34},{34,2},{3,35},{35,3},{4,36},{36... | collective-permute-start | bytes 3538952 | tf_op jit(solution)/shard_map/ppermute | solution.py:223
  78.8 4.5 %all-to-all-start.2 = ((bf16[4,16,48,384]{3,2,1,0:T(8,128)(2,1)}), bf16[4,16,48,384]{3,2,1,0:T(8,128)(2,1)}, u32[]{:S(2)}, u32[]{:S(2)}) async-start(bf16[4,16,48,384]{3,2,1,0:T(8,128)(2,1)} %pad_maximum_fusion), calls=%async_computation.2 | async-start | bytes 4718592 | tf_op jit(solution)/shard_map/all_to_all | solution.py:220
  83.8 7.7 %collective-permute-done.9.refs_6_ = bf16[4,96,1536]{2,1,0:T(8,128)(2,1)S(1)} collective-permute-done((bf16[4,96,1536]{2,1,0:T(8,128)(2,1)S(1)}, bf16[4,96,1536]{2,1,0:T(8,128)(2,1)S(1)}, u32[]{:S(2)}, u32[]{:S(2)}) %collective-permute-start.9) | collective-permute-done | bytes 1179680 | tf_op jit(solution)/shard_map/ppermute | solution.py:205
  91.5 3.0 %collective-permute-done.8.refs_5_ = bf16[4,96,1536]{2,1,0:T(8,128)(2,1)} collective-permute-done((bf16[4,96,1536]{2,1,0:T(8,128)(2,1)S(1)}, bf16[4,96,1536]{2,1,0:T(8,128)(2,1)}, u32[]{:S(2)}, u32[]{:S(2)}) %collective-permute-start.8) | collective-permute-done | bytes 1179680 | tf_op jit(solution)/shard_map/ppermute | solution.py:205
  96.1 1.9 %slice.32 = bf16[2,96,1536]{2,1,0:T(8,128)(2,1)} slice(bf16[4,96,1536]{2,1,0:T(8,128)(2,1)} %collective-permute-done.8.refs_5_), slice={[0:2], [0:96], [0:1536]} | slice | bytes 1179648 | tf_op jit(solution)/shard_map/slice | solution.py:209
  100.8 2.0 %slice.35 = bf16[2,96,1536]{2,1,0:T(8,128)(2,1)} slice(bf16[4,96,1536]{2,1,0:T(8,128)(2,1)} %collective-permute-done.11.refs_10_), slice={[2:4], [0:96], [0:1536]} | slice | bytes 1179648 | tf_op jit(solution)/shard_map/slice | solution.py:209
  102.7 2.1 %collective-permute-start.17 = (bf16[2,96,1536]{2,1,0:T(8,128)(2,1)}, bf16[2,96,1536]{2,1,0:T(8,128)(2,1)}, u32[]{:S(2)}, u32[]{:S(2)}) collective-permute-start(bf16[2,96,1536]{2,1,0:T(8,128)(2,1)} %slice.35), channel_id=1, source_target_pairs={{0,6},{2,0},{4,2},{6,4},{1,7},{3,1},{5,3},{7,5},{8,14},{10,8},{12,... | collective-permute-start | bytes 1769480 | tf_op jit(solution)/shard_map/ppermute | solution.py:209
  106.4 12.0 %contract_first.1.refs_13_ = f32[1536,1536]{1,0:T(8,128)} custom-call(s32[4]{0:T(128)S(1)} %pad_add_fusion.place, bf16[16,2,48,384]{3,2,1,0:T(8,128)(2,1)S(1)} %bitcast.16, bf16[16,2,48,384]{3,2,1,0:T(8,128)(2,1)} %bitcast.8.refs_1_, bf16[16,2,48,384]{3,2,1,0:T(8,128)(2,1)} %bitcast.9.refs_2_, bf16[16,2,48,384]{3,2,1,0:T(8,128)(2,1)} %bitcast.10.refs_3_, ...), custom_call_target="tpu_custom_call" | custom-call | flops 575000000 | bytes 1048576 | tf_op jit(solution)/shard_map/contract_first/pallas_call | solution.py:170
  118.4 2.6 %collective-permute-done.16.refs_11_ = bf16[2,96,1536]{2,1,0:T(8,128)(2,1)} collective-permute-done((bf16[2,96,1536]{2,1,0:T(8,128)(2,1)}, bf16[2,96,1536]{2,1,0:T(8,128)(2,1)}, u32[]{:S(2)}, u32[]{:S(2)}) %collective-permute-start.16) | collective-permute-done | bytes 589856 | tf_op jit(solution)/shard_map/ppermute | solution.py:209
  124.6 4.4 %collective-permute-done.18.refs_5_ = bf16[4,16,48,384]{3,2,1,0:T(8,128)(2,1)S(1)} collective-permute-done((bf16[4,16,48,384]{3,2,1,0:T(8,128)(2,1)}, bf16[4,16,48,384]{3,2,1,0:T(8,128)(2,1)S(1)}, u32[]{:S(2)}, u32[]{:S(2)}) %collective-permute-start.18) | collective-permute-done | bytes 2359328 | tf_op jit(solution)/shard_map/ppermute | solution.py:223
  132.4 18.3 %contract_last.1 = bf16[1536,4,384]{2,1,0:T(4,128)(2,1)} custom-call(s32[4]{0:T(128)S(1)} %pad_add_fusion.place, bf16[16,2,48,384]{3,2,1,0:T(8,128)(2,1)S(1)} %bitcast.17, bf16[16,2,48,384]{3,2,1,0:T(8,128)(2,1)} %bitcast.8.refs_1_, bf16[16,2,48,384]{3,2,1,0:T(8,128)(2,1)} %bitcast.9.refs_2_, bf16[16,2,48,384]{3,2,1,0:T(8,128)(2,1)} %bitcast.10.refs_3_, ...), custom_call_target="tpu_custom_call" | custom-call | flops 13799999488 | bytes 1048576 | tf_op jit(solution)/shard_map/contract_last/pallas_call | solution.py:170
  (49 shorter events, 26.0 us)
Async XLA Ops:
  1.1 13.5 %collective-permute-start = (bf16[2,48,1536]{2,1,0:T(8,128)(2,1)S(1)}, bf16[2,48,1536]{2,1,0:T(8,128)(2,1)S(1)}, u32[]{:S(2)}, u32[]{:S(2)}) collective-permute-start(bf16[2,48,1536]{2,1,0:T(8,128)(2,1)S(1)} %reshape.20), channel_id=1, source_target_pairs={{0,1},{1,0},{2,3},{3,2},{4,5},{5,4},{6,7},{7,6},{8,9},{9,8},{10,11... | collective-permute-start | bytes 884744 | tf_op jit(solution)/shard_map/ppermute | solution.py:226
  6.5 38.7 %all-to-all-start = ((bf16[32,48,384]{2,1,0:T(8,128)(2,1)}), bf16[32,48,384]{2,1,0:T(8,128)(2,1)S(1)}, u32[]{:S(2)}, u32[]{:S(2)}) async-start(bf16[32,48,384]{2,1,0:T(8,128)(2,1)} %bitcast.5), calls=%async_computation | async-start | bytes 2359296 | tf_op jit(solution)/shard_map/all_to_all | solution.py:220
  14.7 22.0 %collective-permute-start.6 = (bf16[1,96,1536]{2,1,0:T(8,128)(2,1)S(1)}, bf16[1,96,1536]{2,1,0:T(8,128)(2,1)S(1)}, u32[]{:S(2)}, u32[]{:S(2)}) collective-permute-start(bf16[1,96,1536]{2,1,0:T(8,128)(2,1)S(1)} %get-tuple-element.57), channel_id=1, source_target_pairs={{0,16},{8,24},{16,0},{24,8},{1,17},{9,25},{17,1},{25,9},{2,18},{10... | collective-permute-start | bytes 884744 | tf_op jit(solution)/shard_map/ppermute | solution.py:200
  17.5 24.7 %collective-permute-start.5 = (bf16[1,96,1536]{2,1,0:T(8,128)(2,1)S(1)}, bf16[1,96,1536]{2,1,0:T(8,128)(2,1)S(1)}, u32[]{:S(2)}, u32[]{:S(2)}) collective-permute-start(bf16[1,96,1536]{2,1,0:T(8,128)(2,1)S(1)} %get-tuple-element.57), channel_id=1, source_target_pairs={{0,24},{8,0},{16,8},{24,16},{1,25},{9,1},{17,9},{25,17},{2,26},{10... | collective-permute-start | bytes 884744 | tf_op jit(solution)/shard_map/ppermute | solution.py:200
  18.4 25.5 %collective-permute-start.4 = (bf16[1,96,1536]{2,1,0:T(8,128)(2,1)S(1)}, bf16[1,96,1536]{2,1,0:T(8,128)(2,1)S(1)}, u32[]{:S(2)}, u32[]{:S(2)}) collective-permute-start(bf16[1,96,1536]{2,1,0:T(8,128)(2,1)S(1)} %get-tuple-element.57), channel_id=1, source_target_pairs={{0,8},{8,16},{16,24},{24,0},{1,9},{9,17},{17,25},{25,1},{2,10},{10... | collective-permute-start | bytes 884744 | tf_op jit(solution)/shard_map/ppermute | solution.py:200
  18.9 26.1 %collective-permute-start.3 = (bf16[1,96,1536]{2,1,0:T(8,128)(2,1)S(1)}, bf16[1,96,1536]{2,1,0:T(8,128)(2,1)S(1)}, u32[]{:S(2)}, u32[]{:S(2)}) collective-permute-start(bf16[1,96,1536]{2,1,0:T(8,128)(2,1)S(1)} %get-tuple-element.58), channel_id=1, source_target_pairs={{0,4},{2,6},{4,0},{6,2},{1,5},{3,7},{5,1},{7,3},{8,12},{10,14},{12... | collective-permute-start | bytes 884744 | tf_op jit(solution)/shard_map/ppermute | solution.py:200
  21.6 23.4 %collective-permute-start.2 = (bf16[1,96,1536]{2,1,0:T(8,128)(2,1)S(1)}, bf16[1,96,1536]{2,1,0:T(8,128)(2,1)S(1)}, u32[]{:S(2)}, u32[]{:S(2)}) collective-permute-start(bf16[1,96,1536]{2,1,0:T(8,128)(2,1)S(1)} %get-tuple-element.58), channel_id=1, source_target_pairs={{0,6},{2,0},{4,2},{6,4},{1,7},{3,1},{5,3},{7,5},{8,14},{10,8},{12,... | collective-permute-start | bytes 884744 | tf_op jit(solution)/shard_map/ppermute | solution.py:200
  36.7 8.3 %collective-permute-start.1 = (bf16[1,96,1536]{2,1,0:T(8,128)(2,1)S(1)}, bf16[1,96,1536]{2,1,0:T(8,128)(2,1)S(1)}, u32[]{:S(2)}, u32[]{:S(2)}) collective-permute-start(bf16[1,96,1536]{2,1,0:T(8,128)(2,1)S(1)} %get-tuple-element.58), channel_id=1, source_target_pairs={{0,2},{2,4},{4,6},{6,0},{1,3},{3,5},{5,7},{7,1},{8,10},{10,12},{12... | collective-permute-start | bytes 884744 | tf_op jit(solution)/shard_map/ppermute | solution.py:200
  45.8 26.9 %collective-permute-start.12 = (bf16[32,48,384]{2,1,0:T(8,128)(2,1)S(1)}, bf16[32,48,384]{2,1,0:T(8,128)(2,1)}, u32[]{:S(2)}, u32[]{:S(2)}) collective-permute-start(bf16[32,48,384]{2,1,0:T(8,128)(2,1)S(1)} %all-to-all-done), channel_id=1, source_target_pairs={{0,64},{64,0},{1,65},{65,1},{2,66},{66,2},{3,67},{67,3},{4,68},{68... | collective-permute-start | bytes 3538952 | tf_op jit(solution)/shard_map/ppermute | solution.py:242
  48.6 20.6 %all-to-all-start.1 = ((bf16[16,2,48,384]{3,2,1,0:T(8,128)(2,1)}), bf16[16,2,48,384]{3,2,1,0:T(8,128)(2,1)}, u32[]{:S(2)}, u32[]{:S(2)}) async-start(bf16[16,2,48,384]{3,2,1,0:T(8,128)(2,1)} %bitcast.6), calls=%async_computation.1 | async-start | bytes 2359296 | tf_op jit(solution)/shard_map/all_to_all | solution.py:220
  53.1 38.4 %collective-permute-start.9 = (bf16[4,96,1536]{2,1,0:T(8,128)(2,1)S(1)}, bf16[4,96,1536]{2,1,0:T(8,128)(2,1)S(1)}, u32[]{:S(2)}, u32[]{:S(2)}) collective-permute-start(bf16[4,96,1536]{2,1,0:T(8,128)(2,1)S(1)} %pad_maximum_fusion.1.refs_4_), channel_id=1, source_target_pairs={{0,24},{8,0},{16,8},{24,16},{1,25},{9,1},{17,9},{25,17},{2,26},{10... | collective-permute-start | bytes 3538952 | tf_op jit(solution)/shard_map/ppermute | solution.py:205
  55.7 38.9 %collective-permute-start.8 = (bf16[4,96,1536]{2,1,0:T(8,128)(2,1)S(1)}, bf16[4,96,1536]{2,1,0:T(8,128)(2,1)}, u32[]{:S(2)}, u32[]{:S(2)}) collective-permute-start(bf16[4,96,1536]{2,1,0:T(8,128)(2,1)S(1)} %pad_maximum_fusion.1.refs_4_), channel_id=1, source_target_pairs={{0,8},{8,16},{16,24},{24,0},{1,9},{9,17},{17,25},{25,1},{2,10},{10... | collective-permute-start | bytes 3538952 | tf_op jit(solution)/shard_map/ppermute | solution.py:205
  55.7 38.9 %collective-permute-start.11 = (bf16[4,96,1536]{2,1,0:T(8,128)(2,1)}, bf16[4,96,1536]{2,1,0:T(8,128)(2,1)}, u32[]{:S(2)}, u32[]{:S(2)}) collective-permute-start(bf16[4,96,1536]{2,1,0:T(8,128)(2,1)} %pad_maximum_fusion.2.refs_8_), channel_id=1, source_target_pairs={{0,6},{2,0},{4,2},{6,4},{1,7},{3,1},{5,3},{7,5},{8,14},{10,8},{12,... | collective-permute-start | bytes 3538952 | tf_op jit(solution)/shard_map/ppermute | solution.py:205
  58.1 36.6 %collective-permute-start.10 = (bf16[4,96,1536]{2,1,0:T(8,128)(2,1)}, bf16[4,96,1536]{2,1,0:T(8,128)(2,1)}, u32[]{:S(2)}, u32[]{:S(2)}) collective-permute-start(bf16[4,96,1536]{2,1,0:T(8,128)(2,1)} %pad_maximum_fusion.2.refs_8_), channel_id=1, source_target_pairs={{0,2},{2,4},{4,6},{6,0},{1,3},{3,5},{5,7},{7,1},{8,10},{10,12},{12... | collective-permute-start | bytes 3538952 | tf_op jit(solution)/shard_map/ppermute | solution.py:205
  72.7 33.4 %collective-permute-start.7 = (bf16[32,48,384]{2,1,0:T(8,128)(2,1)S(1)}, bf16[32,48,384]{2,1,0:T(8,128)(2,1)}, u32[]{:S(2)}, u32[]{:S(2)}) collective-permute-start(bf16[32,48,384]{2,1,0:T(8,128)(2,1)S(1)} %all-to-all-done), channel_id=1, source_target_pairs={{0,32},{32,0},{1,33},{33,1},{2,34},{34,2},{3,35},{35,3},{4,36},{36... | collective-permute-start | bytes 3538952 | tf_op jit(solution)/shard_map/ppermute | solution.py:223
  78.8 44.1 %all-to-all-start.2 = ((bf16[4,16,48,384]{3,2,1,0:T(8,128)(2,1)}), bf16[4,16,48,384]{3,2,1,0:T(8,128)(2,1)}, u32[]{:S(2)}, u32[]{:S(2)}) async-start(bf16[4,16,48,384]{3,2,1,0:T(8,128)(2,1)} %pad_maximum_fusion), calls=%async_computation.2 | async-start | bytes 4718592 | tf_op jit(solution)/shard_map/all_to_all | solution.py:220
  94.6 11.8 %collective-permute-start.13 = (bf16[32,48,384]{2,1,0:T(8,128)(2,1)}, bf16[32,48,384]{2,1,0:T(8,128)(2,1)}, u32[]{:S(2)}, u32[]{:S(2)}) collective-permute-start(bf16[32,48,384]{2,1,0:T(8,128)(2,1)} %collective-permute-done.12), channel_id=1, source_target_pairs={{0,32},{32,0},{1,33},{33,1},{2,34},{34,2},{3,35},{35,3},{4,36},{36... | collective-permute-start | bytes 3538952 | tf_op jit(solution)/shard_map/ppermute | solution.py:223
  102.7 15.7 %collective-permute-start.17 = (bf16[2,96,1536]{2,1,0:T(8,128)(2,1)}, bf16[2,96,1536]{2,1,0:T(8,128)(2,1)}, u32[]{:S(2)}, u32[]{:S(2)}) collective-permute-start(bf16[2,96,1536]{2,1,0:T(8,128)(2,1)} %slice.35), channel_id=1, source_target_pairs={{0,6},{2,0},{4,2},{6,4},{1,7},{3,1},{5,3},{7,5},{8,14},{10,8},{12,... | collective-permute-start | bytes 1769480 | tf_op jit(solution)/shard_map/ppermute | solution.py:209
  104.9 16.2 %collective-permute-start.16 = (bf16[2,96,1536]{2,1,0:T(8,128)(2,1)}, bf16[2,96,1536]{2,1,0:T(8,128)(2,1)}, u32[]{:S(2)}, u32[]{:S(2)}) collective-permute-start(bf16[2,96,1536]{2,1,0:T(8,128)(2,1)} %slice.34), channel_id=1, source_target_pairs={{0,2},{2,4},{4,6},{6,0},{1,3},{3,5},{5,7},{7,1},{8,10},{10,12},{12... | collective-permute-start | bytes 1769480 | tf_op jit(solution)/shard_map/ppermute | solution.py:209
  104.9 16.2 %collective-permute-start.15 = (bf16[2,96,1536]{2,1,0:T(8,128)(2,1)}, bf16[2,96,1536]{2,1,0:T(8,128)(2,1)}, u32[]{:S(2)}, u32[]{:S(2)}) collective-permute-start(bf16[2,96,1536]{2,1,0:T(8,128)(2,1)} %slice.33), channel_id=1, source_target_pairs={{0,24},{8,0},{16,8},{24,16},{1,25},{9,1},{17,9},{25,17},{2,26},{10... | collective-permute-start | bytes 1769480 | tf_op jit(solution)/shard_map/ppermute | solution.py:209
  106.0 15.5 %collective-permute-start.14 = (bf16[2,96,1536]{2,1,0:T(8,128)(2,1)}, bf16[2,96,1536]{2,1,0:T(8,128)(2,1)}, u32[]{:S(2)}, u32[]{:S(2)}) collective-permute-start(bf16[2,96,1536]{2,1,0:T(8,128)(2,1)} %slice.32), channel_id=1, source_target_pairs={{0,8},{8,16},{16,24},{24,0},{1,9},{9,17},{17,25},{25,1},{2,10},{10... | collective-permute-start | bytes 1769480 | tf_op jit(solution)/shard_map/ppermute | solution.py:209
  122.8 6.1 %collective-permute-start.18 = (bf16[4,16,48,384]{3,2,1,0:T(8,128)(2,1)}, bf16[4,16,48,384]{3,2,1,0:T(8,128)(2,1)S(1)}, u32[]{:S(2)}, u32[]{:S(2)}) collective-permute-start(bf16[4,16,48,384]{3,2,1,0:T(8,128)(2,1)} %all-to-all-done.2.refs_4_), channel_id=1, source_target_pairs={{0,32},{32,0},{1,33},{33,1},{2,34},{34,2},{3,35},{35,3},{4,36},{36... | collective-permute-start | bytes 7077896 | tf_op jit(solution)/shard_map/ppermute | solution.py:223
  129.0 1.5 copy-start.3
  130.4 1.3 copy-start
  (2 other events, 1.3 us)
